TPU v7x, 256 devices: a whole 4x4x8 slice. The times are simulated.
256 devices in a mesh: grp: 4 (over y_lo, core), resp: 8 (over x, y_hi), head: 8 (over z).
Axes of the slice: x: 4, y: 4 (y_hi: 2, y_lo: 2; y = y_hi * 2 + y_lo), z: 8, core: 2. Of those that a mesh axis runs over, the one named last changes fastest.
Arguments:
- resp_hidden: bfloat16 [32, 128, 5120], P(('grp', 'resp')), parts along dimension 0, may hold values from -6 to 6
- prompt_hidden: bfloat16 [4096, 5120], P(('grp', 'resp')), parts along dimension 0, may hold values from -6 to 6
- readout: bfloat16 [32, 128, 5120], P(('grp', 'resp')), parts along dimension 0, may hold values from -0.078125 to 0.078125
- query_weight: bfloat16 [5120, 8192], P('resp', 'head'), may hold values from -0.078125 to 0.078125
- key_weight: bfloat16 [5120, 1024], P('resp', 'head'), may hold values from -0.078125 to 0.078125
- value_weight: bfloat16 [5120, 1024], P('resp', 'head'), may hold values from -0.078125 to 0.078125
- out_weight: bfloat16 [5120, 8192], P('resp', 'head'), may hold values from -0.0625 to 0.0625
- query_gain: float32 [128], replicated, may hold values from 0.25 to 1.75
- key_gain: float32 [128], replicated, may hold values from 0.25 to 1.75
- base_logprob: float32 [32, 128], P(('grp', 'resp')), parts along dimension 0, may hold values from -3 to -0.5
- behavior_logprob: float32 [32, 128], P(('grp', 'resp')), parts along dimension 0, may hold values from -4 to 0.5
- reference_logprob: float32 [32, 128], P(('grp', 'resp')), parts along dimension 0, may hold values from -3 to -0.5
- rewards: float32 [32], P(('grp', 'resp')), parts along dimension 0, may hold values from 0.3 to 15.3, as said below
- lengths: int32 [32], P(('grp', 'resp')), parts along dimension 0, may hold values from 1 to 128, as said below
Outputs:
- policy_logprob: float32 [32, 128], P(('grp', 'resp')), parts along dimension 0
- group_loss: float32 [4], P('grp'), parts along dimension 0
- query_grad: bfloat16 [20480, 8192], P(('grp', 'resp'), 'head'), parts along dimension 0
- key_grad: bfloat16 [20480, 1024], P(('grp', 'resp'), 'head'), parts along dimension 0
- value_grad: bfloat16 [20480, 1024], P(('grp', 'resp'), 'head'), parts along dimension 0
- out_grad: bfloat16 [20480, 8192], P(('grp', 'resp'), 'head'), parts along dimension 0
There are 4 independent parts, one for each index of `grp`. A program takes and returns all parts, laid end to end along the dimension named above; an argument that names none is the same for every part. Nothing has to cross between parts.
Inputs may be any that keep to these rules, and one draw needn't show every extreme that they name: `lengths`: a response's live tokens come first; later positions are padding. `rewards`: scalar reward of a response.
All inputs are finite; a program needn't handle non-finite values.
Results may differ from a plain program's by a relative error of at most 0.023.
Values may be sent and summed in bfloat16 or wider, within the bound.
No kernel may reach another device: no remote copies, remote signals or barrier semaphores. Data moves between devices by JAX's collectives and lax.ppermute only.
A program may use at most 128 MiB of HBM per device.

v0:
```python
import math

import jax
import jax.numpy as jnp
from jax import lax
from jax.sharding import PartitionSpec as P

HD = 128


norm_eps = 1e-06
rope_base = 1000000.0
clip_low = 0.8
clip_high = 1.28
kl_weight = 0.04


def norm_rope(values, scale_gain, positions):
    row_count = values.shape[0]
    head_count = values.shape[1] // HD
    shaped = values.reshape(row_count, head_count, HD)
    mean_square = jnp.mean(shaped * shaped, axis=-1, keepdims=True)
    normed = shaped * lax.rsqrt(mean_square + norm_eps) * scale_gain
    half_dim = HD // 2
    frequency = jnp.exp(jnp.arange(half_dim, dtype=jnp.float32) * (-2.0 * math.log(rope_base) / HD))
    angles = positions[:, None] * frequency[None, :]
    cosine_table = jnp.cos(angles)[:, None, :]
    sine_table = jnp.sin(angles)[:, None, :]
    first_half = normed[..., :half_dim]
    second_half = normed[..., half_dim:]
    rotated = jnp.concatenate(
        [
            first_half * cosine_table - second_half * sine_table,
            second_half * cosine_table + first_half * sine_table,
        ],
        axis=-1,
    )
    return rotated.reshape(row_count, head_count * HD)


def rope_back(pre_values, scale_gain, positions, cotangent):
    result = jax.vjp(
        lambda inner_values: norm_rope(inner_values, scale_gain, positions), pre_values
    )[1](cotangent)
    return result[0]


def seen_mask(query_count, key_count, prompt_count):
    query_index = jnp.arange(query_count)[:, None]
    key_index = jnp.arange(key_count)[None, :]
    return (key_index < prompt_count) | (key_index - prompt_count <= query_index)


def split_heads(query, keys, values):
    row_count = query.shape[0]
    key_count = keys.shape[0]
    kv_heads = keys.shape[1] // HD
    group_size = query.shape[1] // keys.shape[1]
    query_heads = query.reshape(row_count, kv_heads, group_size, HD)
    key_heads = keys.reshape(key_count, kv_heads, HD)
    value_heads = values.reshape(key_count, kv_heads, HD)
    return (query_heads, key_heads, value_heads)


def attend(query, keys, values, prompt_count):
    query_heads, key_heads, value_heads = split_heads(query, keys, values)
    row_count = query.shape[0]
    scores = jnp.einsum(
        "tkgh,nkh->kgtn", query_heads, key_heads, preferred_element_type=jnp.float32
    ) * HD ** (-0.5)
    weights = jnp.where(seen_mask(row_count, keys.shape[0], prompt_count), jnp.exp(scores), 0.0)
    probs = weights / jnp.sum(weights, axis=-1, keepdims=True)
    probs_low = probs.astype(jnp.bfloat16)
    mixed = jnp.einsum("kgtn,nkh->tkgh", probs_low, value_heads, preferred_element_type=jnp.float32)
    return (mixed.reshape(row_count, -1).astype(jnp.bfloat16), probs, probs_low)


def attend_back(query, keys, values, probs, probs_low, grad_low):
    query_heads, key_heads, value_heads = split_heads(query, keys, values)
    row_count = query.shape[0]
    key_count = keys.shape[0]
    grad_heads = grad_low.reshape(query_heads.shape)
    value_cot = jnp.einsum(
        "kgtn,tkgh->nkh", probs_low, grad_heads, preferred_element_type=jnp.float32
    )
    prob_cot = jnp.einsum(
        "tkgh,nkh->kgtn", grad_heads, value_heads, preferred_element_type=jnp.float32
    )
    inner_sum = jnp.sum(probs * prob_cot, axis=-1, keepdims=True)
    score_cot = (probs * (prob_cot - inner_sum) * HD ** (-0.5)).astype(jnp.bfloat16)
    query_cot = jnp.einsum(
        "kgtn,nkh->tkgh", score_cot, key_heads, preferred_element_type=jnp.float32
    ).reshape(row_count, -1)
    key_cot = jnp.einsum(
        "kgtn,tkgh->nkh", score_cot, query_heads, preferred_element_type=jnp.float32
    ).reshape(key_count, -1)
    return (query_cot, key_cot, value_cot.reshape(key_count, -1))


def objective(logprob, behavior, reference_lp, advantage, live):
    ratios = jnp.exp(logprob - behavior)
    weight = jnp.clip(ratios, clip_low, clip_high)
    ref_gap = reference_lp - logprob
    penalty = jnp.exp(ref_gap) - ref_gap - 1.0
    token_loss = live * (kl_weight * penalty - weight * advantage * logprob)
    lp_slope = live * (kl_weight * (1.0 - jnp.exp(ref_gap)) - weight * advantage)
    return (jnp.sum(token_loss), lp_slope)


def token_cols(own_x, prompt_hidden, own_read):
    return (
        lax.all_to_all(own_x, "resp", split_axis=1, concat_axis=0, tiled=True),
        lax.all_to_all(prompt_hidden, "resp", split_axis=1, concat_axis=0, tiled=True),
        lax.all_to_all(own_read, "resp", split_axis=1, concat_axis=0, tiled=True),
    )


def body(
    resp_hidden,
    prompt_hidden,
    readout,
    query_weight,
    key_weight,
    value_weight,
    out_weight,
    query_gain,
    key_gain,
    base_logprob,
    behavior_logprob,
    reference_logprob,
    rewards,
    lengths,
):
    own_x = resp_hidden[0]
    own_read = readout[0]
    row_total = own_x.shape[0]
    prompt_rows = prompt_hidden.shape[0]
    qcols_dev = query_weight.shape[1]
    kcols_dev = key_weight.shape[1]
    groups = lax.axis_size("resp")
    index = lax.axis_index("resp")
    columns = None
    columns = token_cols(own_x, prompt_hidden, own_read)
    cols_x, cols_p, cols_r = columns
    partial_terms = (
        jnp.dot(cols_x, query_weight, preferred_element_type=jnp.float32),
        jnp.dot(cols_x, key_weight, preferred_element_type=jnp.float32),
        jnp.dot(cols_x, value_weight, preferred_element_type=jnp.float32),
        jnp.dot(cols_p, key_weight, preferred_element_type=jnp.float32),
        jnp.dot(cols_p, value_weight, preferred_element_type=jnp.float32),
        jnp.dot(cols_r, out_weight, preferred_element_type=jnp.float32),
    )
    q_pre, kr_pre, vr_pre, kp_pre, vp_pre, mixing = (
        lax.psum_scatter(partial_terms[0], "resp", scatter_dimension=0, tiled=True),
        lax.psum_scatter(partial_terms[1], "resp", scatter_dimension=0, tiled=True),
        lax.psum_scatter(partial_terms[2], "resp", scatter_dimension=0, tiled=True),
        lax.psum_scatter(partial_terms[3], "resp", scatter_dimension=0, tiled=True),
        lax.psum_scatter(partial_terms[4], "resp", scatter_dimension=0, tiled=True),
        lax.psum_scatter(partial_terms[5], "resp", scatter_dimension=0, tiled=True),
    )
    prompt_pos = (index * prompt_rows + jnp.arange(prompt_rows)).astype(jnp.float32)
    resp_pos = (prompt_rows * groups + jnp.arange(row_total)).astype(jnp.float32)
    prompt_keys = norm_rope(kp_pre, key_gain, prompt_pos).astype(jnp.bfloat16)
    prompt_values = vp_pre.astype(jnp.bfloat16)
    every_key, every_value = (
        lax.all_gather(prompt_keys, "resp", axis=0, tiled=True),
        lax.all_gather(prompt_values, "resp", axis=0, tiled=True),
    )
    prompt_count = every_key.shape[0]
    query = norm_rope(q_pre, query_gain, resp_pos).astype(jnp.bfloat16)
    resp_keys = norm_rope(kr_pre, key_gain, resp_pos).astype(jnp.bfloat16)
    keys = jnp.concatenate([every_key, resp_keys], axis=0)
    values = jnp.concatenate([every_value, vr_pre.astype(jnp.bfloat16)], axis=0)
    mixed, probs, probs_low = attend(query, keys, values, prompt_count)
    mixed_wide = mixed.astype(jnp.float32)
    attn_part = jnp.sum(mixed_wide * mixing, axis=-1)
    own_part = jnp.einsum("td,td->t", own_x, own_read, preferred_element_type=jnp.float32)
    reward_sum = lax.psum(rewards, "resp")[0]
    attn_logit = lax.psum(attn_part, "head")
    logprob = base_logprob[0] + own_part + attn_logit
    advantage = rewards[0] - reward_sum / groups
    live = (jnp.arange(row_total) < lengths[0]).astype(jnp.float32)
    loss_own, lp_slope = objective(
        logprob, behavior_logprob[0], reference_logprob[0], advantage, live
    )
    group_loss = lax.psum(loss_own, "resp").reshape(1)
    mixed_grad = (lp_slope[:, None] * mixing).astype(jnp.bfloat16)
    mixing_grad = (lp_slope[:, None] * mixed_wide).astype(jnp.bfloat16)
    query_cot, key_cot, value_cot = attend_back(query, keys, values, probs, probs_low, mixed_grad)
    dkp_own, dvp_own = (
        lax.psum_scatter(
            key_cot[:prompt_count].astype(jnp.bfloat16), "resp", scatter_dimension=0, tiled=True
        ).astype(jnp.float32),
        lax.psum_scatter(
            value_cot[:prompt_count].astype(jnp.bfloat16), "resp", scatter_dimension=0, tiled=True
        ).astype(jnp.float32),
    )
    dkp_low = rope_back(kp_pre, key_gain, prompt_pos, dkp_own).astype(jnp.bfloat16)
    dvp_low = dvp_own.astype(jnp.bfloat16)
    dq_low = rope_back(q_pre, query_gain, resp_pos, query_cot).astype(jnp.bfloat16)
    dkr_low = rope_back(kr_pre, key_gain, resp_pos, key_cot[prompt_count:]).astype(jnp.bfloat16)
    dvr_low = value_cot[prompt_count:].astype(jnp.bfloat16)
    cols_x, cols_p, cols_r = columns
    every_dq, every_dkr, every_dvr, every_dkp, every_dvp, every_mix = (
        lax.all_gather(dq_low, "resp", axis=0, tiled=True),
        lax.all_gather(dkr_low, "resp", axis=0, tiled=True),
        lax.all_gather(dvr_low, "resp", axis=0, tiled=True),
        lax.all_gather(dkp_low, "resp", axis=0, tiled=True),
        lax.all_gather(dvp_low, "resp", axis=0, tiled=True),
        lax.all_gather(mixing_grad, "resp", axis=0, tiled=True),
    )
    slice_width = cols_x.shape[1]
    src_x = cols_x.reshape(groups, row_total, slice_width)
    src_p = cols_p.reshape(groups, prompt_rows, slice_width)
    src_r = cols_r.reshape(groups, row_total, slice_width)

    def by_source(left, right, row_count):
        shaped = right.reshape(groups, row_count, right.shape[1])
        return jnp.einsum("ntd,ntc->ndc", left, shaped, preferred_element_type=jnp.float32)

    per_source = jnp.concatenate(
        [
            by_source(src_x, every_dq, row_total),
            by_source(src_x, every_dkr, row_total) + by_source(src_p, every_dkp, prompt_rows),
            by_source(src_x, every_dvr, row_total) + by_source(src_p, every_dvp, prompt_rows),
            by_source(src_r, every_mix, row_total),
        ],
        axis=2,
    )
    summed = jnp.sum(
        lax.optimization_barrier(per_source.astype(jnp.bfloat16)).astype(jnp.float32), axis=0
    )
    k_end = qcols_dev + kcols_dev
    v_end = k_end + kcols_dev
    return (
        logprob[None, :],
        group_loss,
        summed[:, :qcols_dev].astype(jnp.bfloat16),
        summed[:, qcols_dev:k_end].astype(jnp.bfloat16),
        summed[:, k_end:v_end].astype(jnp.bfloat16),
        summed[:, v_end:].astype(jnp.bfloat16),
    )


def solution(mesh):
    placed = (
        P(("grp", "resp"), None, None),
        P(("grp", "resp"), None),
        P(("grp", "resp"), None, None),
        P("resp", "head"),
        P("resp", "head"),
        P("resp", "head"),
        P("resp", "head"),
        P(),
        P(),
        P(("grp", "resp"), None),
        P(("grp", "resp"), None),
        P(("grp", "resp"), None),
        P(("grp", "resp")),
        P(("grp", "resp")),
    )
    return jax.shard_map(
        body,
        mesh=mesh,
        in_specs=placed,
        out_specs=(
            P(("grp", "resp"), None),
            P("grp"),
            P(("grp", "resp"), "head"),
            P(("grp", "resp"), "head"),
            P(("grp", "resp"), "head"),
            P(("grp", "resp"), "head"),
        ),
        check_vma=False,
    )
```

profile of v0, /device:TPU:2, one launch (start us, length us, event | category | flops | bytes accessed | tf_op | source)
XLA Modules:
  0.0 916.9 jit_solution(1332993971764567169)
XLA Ops:
  22.9 13.0 %all-to-all-done = bf16[128,8,640]{2,0,1:T(8,128)(2,1)S(1)} async-done(((bf16[128,8,640]{2,0,1:T(8,128)(2,1)}), bf16[128,8,640]{2,0,1:T(8,128)(2,1)S(1)}, u32[]{:S(2)}, u32[]{:S(2)}) %all-to-all-start) | async-done | bytes 1310752 | tf_op jit(solution)/shard_map/all_to_all | solution.py:113
  45.2 14.1 %all-to-all-done.1 = bf16[128,8,640]{2,0,1:T(8,128)(2,1)S(1)} async-done(((bf16[128,8,640]{2,0,1:T(8,128)(2,1)}), bf16[128,8,640]{2,0,1:T(8,128)(2,1)S(1)}, u32[]{:S(2)}, u32[]{:S(2)}) %all-to-all-start.1) | async-done | bytes 1310752 | tf_op jit(solution)/shard_map/all_to_all | solution.py:112
  73.0 23.1 %all_to_all.57 = bf16[128,8,640]{2,0,1:T(8,128)(2,1)S(1)} all-to-all(bf16[128,8,640]{2,0,1:T(8,128)(2,1)S(1)} %copy.188), channel_id=1, replica_groups=mesh['grp'=4,'resp'=8,'head'=8] {'resp'}, dimensions={1} | all-to-all | bytes 2621440 | tf_op jit(solution)/shard_map/all_to_all | solution.py:114
  101.1 20.3 %psum.22 = f32[1]{0:T(128)} all-reduce(f32[1]{0:T(128)} %param.26), channel_id=1, replica_groups=mesh['grp'=4,'resp'=8,'head'=8] {'resp'}, use_global_device_ids=true, to_apply=%region_12.13 | all-reduce | flops 1 | bytes 8 | tf_op jit(solution)/shard_map/psum | solution.py:178
  128.8 78.4 %reduce-scatter.13.cloned.1.call-done = f32[128,128]{1,0:T(8,128)} async-done(((f32[1024,128]{1,0:T(8,128)}), f32[128,128]{1,0:T(8,128)}) %reduce-scatter.13.cloned.1.call-update) | async-done | bytes 65552 | tf_op jit(solution)/shard_map/reduce_scatter | solution.py:156
  208.1 77.9 %reduce-scatter.15.cloned.1.call-done = f32[128,128]{1,0:T(8,128)} async-done(((f32[1024,128]{1,0:T(8,128)}), f32[128,128]{1,0:T(8,128)}) %reduce-scatter.15.cloned.1.call-update) | async-done | bytes 65552 | tf_op jit(solution)/shard_map/reduce_scatter | solution.py:157
  286.9 78.2 %reduce-scatter.17.cloned.1.call-done = f32[128,128]{1,0:T(8,128)} async-done(((f32[1024,128]{1,0:T(8,128)}), f32[128,128]{1,0:T(8,128)}) %reduce-scatter.17.cloned.1.call-update) | async-done | bytes 65552 | tf_op jit(solution)/shard_map/reduce_scatter | solution.py:155
  367.9 32.9 %all_gather.24 = bf16[1024,128]{1,0:T(8,128)(2,1)S(1)} all-gather(bf16[128,128]{1,0:T(8,128)(2,1)S(1)} %convert_element_type.134), channel_id=1, replica_groups=mesh['grp'=4,'resp'=8,'head'=8] {'resp'}, dimensions={0}, use_global_device_ids=true | all-gather | bytes 294912 | tf_op jit(solution)/shard_map/all_gather | solution.py:167
  400.8 34.9 %all-gather = bf16[1024,1,128]{2,0,1:T(8,128)(2,1)S(1)} all-gather(bf16[128,1,128]{2,0,1:T(8,128)(2,1)S(1)} %pad_maximum_fusion.4), channel_id=2, replica_groups=mesh['grp'=4,'resp'=8,'head'=8] {'resp'}, dimensions={0}, use_global_device_ids=true | all-gather | bytes 294912 | tf_op jit(solution)/shard_map/all_gather | solution.py:166
  435.7 26.0 %reduce-scatter.19.cloned.1.call-done = f32[128,1024]{1,0:T(8,128)} async-done(((f32[1024,1024]{1,0:T(8,128)}), f32[128,1024]{1,0:T(8,128)}) %reduce-scatter.19.cloned.1.call-update) | async-done | bytes 524304 | tf_op jit(solution)/shard_map/reduce_scatter | solution.py:154
  476.9 77.6 %reduce-scatter.21.cloned.1.call-done = f32[128,1024]{1,0:T(8,128)} async-done(((f32[1024,1024]{1,0:T(8,128)}), f32[128,1024]{1,0:T(8,128)}) %reduce-scatter.21.cloned.1.call-update) | async-done | bytes 524304 | tf_op jit(solution)/shard_map/reduce_scatter | solution.py:159
  555.7 17.5 %psum.21 = f32[128]{0:T(128)S(1)} all-reduce(f32[128]{0:T(128)S(1)} %multiply_reduce_fusion), channel_id=1, replica_groups=mesh['grp'=4,'resp'=8,'head'=8] {'head'}, use_global_device_ids=true, to_apply=%region_11.12 | all-reduce | flops 128 | bytes 1024 | tf_op jit(solution)/shard_map/psum | solution.py:179
  593.7 20.1 %psum.23 = f32[1]{0:T(128)} all-reduce(f32[1]{0:T(128)} %bitcast.31), channel_id=1, replica_groups=mesh['grp'=4,'resp'=8,'head'=8] {'resp'}, use_global_device_ids=true, to_apply=%region_14.15 | all-reduce | flops 1 | bytes 8 | tf_op jit(solution)/shard_map/psum | solution.py:186
  613.9 31.8 %all-gather.3 = bf16[1024,1,128]{0,2,1:T(8,128)(2,1)S(1)} all-gather(bf16[128,1,128]{0,2,1:T(8,128)(2,1)S(1)} %slice.73), channel_id=5, replica_groups=mesh['grp'=4,'resp'=8,'head'=8] {'resp'}, dimensions={0}, use_global_device_ids=true | all-gather | bytes 294912 | tf_op jit(solution)/shard_map/all_gather | solution.py:207
  658.5 32.7 %all-gather.2 = bf16[1024,1,128]{2,0,1:T(8,128)(2,1)S(1)} all-gather(bf16[128,1,128]{2,0,1:T(8,128)(2,1)S(1)} %get-tuple-element.54), channel_id=4, replica_groups=mesh['grp'=4,'resp'=8,'head'=8] {'resp'}, dimensions={0}, use_global_device_ids=true | all-gather | bytes 294912 | tf_op jit(solution)/shard_map/all_gather | solution.py:208
  691.2 34.7 %all-gather.1 = bf16[1024,1,128]{2,0,1:T(8,128)(2,1)S(1)} all-gather(bf16[128,1,128]{2,0,1:T(8,128)(2,1)S(1)} %get-tuple-element.55), channel_id=3, replica_groups=mesh['grp'=4,'resp'=8,'head'=8] {'resp'}, dimensions={0}, use_global_device_ids=true | all-gather | bytes 294912 | tf_op jit(solution)/shard_map/all_gather | solution.py:206
  725.8 8.8 reduce-scatter.25.cloned.1.call-done
  734.7 33.2 %all_gather.30 = bf16[1024,128]{1,0:T(8,128)(2,1)S(1)} all-gather(bf16[128,128]{1,0:T(8,128)(2,1)} %reduce-scatter.25.cloned.1.call-done), channel_id=1, replica_groups=mesh['grp'=4,'resp'=8,'head'=8] {'resp'}, dimensions={0}, use_global_device_ids=true | all-gather | bytes 294912 | tf_op jit(solution)/shard_map/all_gather | solution.py:209
  771.8 27.3 %all-gather.7.cloned.1.call-done = bf16[1024,1024]{0,1:T(8,128)(2,1)} async-done(((bf16[128,1024]{0,1:T(8,128)(2,1)}), bf16[1024,1024]{0,1:T(8,128)(2,1)}) %all-gather.7.cloned.1.call-update) | async-done | bytes 2097168 | tf_op jit(solution)/shard_map/all_gather | solution.py:205
  803.0 8.4 convert_bitcast_fusion.1
  811.4 49.1 %all-gather.9.cloned.1.call-done = bf16[1024,1024]{1,0:T(8,128)(2,1)} async-done(((bf16[128,1024]{1,0:T(8,128)(2,1)}), bf16[1024,1024]{1,0:T(8,128)(2,1)}) %all-gather.9.cloned.1.call-update) | async-done | bytes 2097168 | tf_op jit(solution)/shard_map/all_gather | solution.py:210
  860.6 8.9 convert_bitcast_fusion
  869.5 16.3 %pad_maximum_fusion = bf16[8,640,2304]{1,2,0:T(8,128)(2,1)} fusion(bf16[8,640,1024]{1,2,0:T(8,128)(2,1)} %convert_bitcast_fusion, bf16[8,640,128]{1,2,0:T(8,128)(2,1)S(1)} %copy-done.9, bf16[8,640,128]{1,2,0:T(8,128)(2,1)S(1)} %copy-done.10, bf16[8,640,1024]{1,2,0:T(8,128)(2,1)} %convert_bitcast_fusion.1), kind=kLoop, calls=%fused_computation | loop fusion | flops 94371840 | bytes 47185920 | tf_op jit(solution)/shard_map/concatenate | solution.py:221
  885.8 14.6 %reduce.8 = bf16[640,2304]{0,1:T(8,128)(2,1)} reduce(bf16[8,640,2304]{1,2,0:T(8,128)(2,1)} %pad_maximum_fusion, bf16[]{:T(256)} %constant.68), dimensions={0}, to_apply=%region_21.22.clone | reduce | flops 10321920 | bytes 26542082 | tf_op jit(solution)/shard_map/reduce_sum | solution.py:230
  (204 shorter events, 120.3 us)
Async XLA Ops:
  7.2 57.6 %copy-start = (bf16[640,1024]{1,0:T(8,128)(2,1)S(1)}, bf16[640,1024]{1,0:T(8,128)(2,1)}, u32[]{:S(2)}) copy-start(bf16[640,1024]{1,0:T(8,128)(2,1)} %param.17) | copy-start | bytes 3932164
  10.5 25.3 %all-to-all-start = ((bf16[128,8,640]{2,0,1:T(8,128)(2,1)}), bf16[128,8,640]{2,0,1:T(8,128)(2,1)S(1)}, u32[]{:S(2)}, u32[]{:S(2)}) async-start(bf16[128,8,640]{2,0,1:T(8,128)(2,1)} %copy.180), calls=%async_computation | async-start | bytes 2621440 | tf_op jit(solution)/shard_map/all_to_all | solution.py:113
  36.9 22.4 %all-to-all-start.1 = ((bf16[128,8,640]{2,0,1:T(8,128)(2,1)}), bf16[128,8,640]{2,0,1:T(8,128)(2,1)S(1)}, u32[]{:S(2)}, u32[]{:S(2)}) async-start(bf16[128,8,640]{2,0,1:T(8,128)(2,1)} %copy.182), calls=%async_computation.2 | async-start | bytes 2621440 | tf_op jit(solution)/shard_map/all_to_all | solution.py:112
  42.5 85.5 %reduce-scatter.11.cloned.1.call-start = ((), (), s32[]{:S(2)}) async-start(), calls=%async_computation.11 | async-start | bytes 589824 | tf_op jit(solution)/shard_map/reduce_scatter | solution.py:158
  45.2 162.1 %reduce-scatter.13.cloned.1.call-start = ((), (), s32[]{:S(2)}) async-start(), calls=%async_computation.12 | async-start | bytes 589824 | tf_op jit(solution)/shard_map/reduce_scatter | solution.py:156
  60.6 225.4 %reduce-scatter.15.cloned.1.call-start = ((), (), s32[]{:S(2)}) async-start(), calls=%async_computation.13 | async-start | bytes 589824 | tf_op jit(solution)/shard_map/reduce_scatter | solution.py:157
  63.4 301.7 %reduce-scatter.17.cloned.1.call-start = ((), (), s32[]{:S(2)}) async-start(), calls=%async_computation.14 | async-start | bytes 589824 | tf_op jit(solution)/shard_map/reduce_scatter | solution.py:155
  64.7 396.9 %reduce-scatter.19.cloned.1.call-start = ((), (), s32[]{:S(2)}) async-start(), calls=%async_computation.15 | async-start | bytes 4718592 | tf_op jit(solution)/shard_map/reduce_scatter | solution.py:154
  68.6 485.9 %reduce-scatter.21.cloned.1.call-start = ((), (), s32[]{:S(2)}) async-start(), calls=%async_computation.16 | async-start | bytes 4718592 | tf_op jit(solution)/shard_map/reduce_scatter | solution.py:159
  101.0 265.1 %copy-start.28 = (f32[128]{0:T(128)S(1)}, f32[128]{0:T(128)}, u32[]{:S(2)}) copy-start(f32[128]{0:T(128)} %param.22) | copy-start | bytes 1540
  101.0 554.7 %reduce-scatter.23.cloned.1.call-start = ((), (), s32[]{:S(2)}) async-start(), calls=%async_computation.18 | async-start | bytes 294912 | tf_op jit(solution)/shard_map/reduce_scatter | solution.py:191
  123.3 244.3 %copy-start.32 = (f32[128]{0:T(128)}, f32[128]{0:T(128)S(1)}, u32[]{:S(2)}) copy-start(f32[128]{0:T(128)S(1)} %get-tuple-element.68) | copy-start | bytes 1540
  123.3 339.5 %copy-start.26 = (f32[128]{0:T(128)}, f32[128]{0:T(128)S(1)}, u32[]{:S(2)}) copy-start(f32[128]{0:T(128)S(1)} %get-tuple-element.67) | copy-start | bytes 1540
  123.7 340.7 %copy-start.23 = (f32[128,64]{1,0:T(8,128)}, f32[128,64]{1,0:T(8,128)S(1)}, u32[]{:S(2)}) copy-start(f32[128,64]{1,0:T(8,128)S(1)} %get-tuple-element.53) | copy-start | bytes 98308
  125.5 337.6 %copy-start.30 = (f32[128]{0:T(128)S(1)}, f32[128]{0:T(128)}, u32[]{:S(2)}) copy-start(f32[128]{0:T(128)} %param.21) | copy-start | bytes 1540
  286.9 79.1 %copy-start.43 = (f32[128]{0:T(128)}, f32[128]{0:T(128)S(1)}, u32[]{:S(2)}) copy-start(f32[128]{0:T(128)S(1)} %multiply_reduce_fusion.3) | copy-start | bytes 1540
  367.9 96.8 %copy-start.24 = (bf16[128,128]{1,0:T(8,128)(2,1)}, bf16[128,128]{1,0:T(8,128)(2,1)S(1)}, u32[]{:S(2)}) copy-start(bf16[128,128]{1,0:T(8,128)(2,1)S(1)} %maximum_bitcast_fusion.6) | copy-start | bytes 98308
  474.5 98.7 %copy-start.34 = (f32[1,128]{1,0:T(1,128)S(1)}, f32[1,128]{1,0:T(1,128)}, u32[]{:S(2)}) copy-start(f32[1,128]{1,0:T(1,128)} %param.25) | copy-start | bytes 1540
  474.5 98.7 %copy-start.36 = (f32[1,128]{1,0:T(1,128)S(1)}, f32[1,128]{1,0:T(1,128)}, u32[]{:S(2)}) copy-start(f32[1,128]{1,0:T(1,128)} %param.24) | copy-start | bytes 1540
  474.5 98.7 %copy-start.47 = (f32[1,128]{1,0:T(1,128)S(1)}, f32[1,128]{1,0:T(1,128)}, u32[]{:S(2)}) copy-start(f32[1,128]{1,0:T(1,128)} %param.23) | copy-start | bytes 1540
  584.4 150.3 %reduce-scatter.25.cloned.1.call-start = ((), (), s32[]{:S(2)}) async-start(), calls=%async_computation.20 | async-start | bytes 294912 | tf_op jit(solution)/shard_map/reduce_scatter | solution.py:194
  589.1 210.0 %all-gather.7.cloned.1.call-start = ((), (), s32[]{:S(2)}) async-start(), calls=%async_computation.17 | async-start | bytes 2359296 | tf_op jit(solution)/shard_map/all_gather | solution.py:205
  593.0 267.6 %all-gather.9.cloned.1.call-start = ((), (), s32[]{:S(2)}) async-start(), calls=%async_computation.19 | async-start | bytes 2359296 | tf_op jit(solution)/shard_map/all_gather | solution.py:210
  691.2 77.3 %copy-start.4 = (bf16[128,8,640]{2,0,1:T(8,128)(2,1)S(1)}, bf16[128,8,640]{2,0,1:T(8,128)(2,1)}, u32[]{:S(2)}) copy-start(bf16[128,8,640]{2,0,1:T(8,128)(2,1)} %copy-done.3) | copy-start | bytes 3932164
  (39 other events, 304.3 us)
Sparse Core Ops, SparseCore 0:
  47.1 80.8 reduce-scatter.10
  132.4 74.8 reduce-scatter.12
  211.1 74.8 reduce-scatter.14
  290.2 74.8 reduce-scatter.16
  369.1 92.5 reduce-scatter.18
  465.7 88.7 reduce-scatter.20
  584.5 71.2 reduce-scatter.22
  660.1 74.5 reduce-scatter.24
  737.2 61.9 all-gather.6
  801.6 58.9 all-gather.8
where the time goes:
time: 919 us; the launch traced here: 917 us
  waiting for transfers between devices  460 us (50%)
  blocking collectives  281 us (31%)
  other arithmetic  55.5 us (6%)
  matrix products  49.6 us (5%)
  local copies, waits for them, and re-layouts  40.4 us (4%)
  between operations  16.9 us (2%)
  starting transfers between devices  13.4 us (1%)
    reduce_scatter x1, waiting for transfers between devices, body(): lax.psum_scatter(partial_terms[2], 'resp', scatter_dimension=0, tiled=True)  78.4 us
    reduce_scatter x1, waiting for transfers between devices, body(): lax.psum_scatter(partial_terms[1], 'resp', scatter_dimension=0, tiled=True)  78.2 us
    reduce_scatter x1, waiting for transfers between devices, body(): lax.psum_scatter(partial_terms[3], 'resp', scatter_dimension=0, tiled=True)  77.9 us
    reduce_scatter x1, waiting for transfers between devices, body(): lax.psum_scatter(partial_terms[5], 'resp', scatter_dimension=0, tiled=True)  77.6 us
    all_gather x1, waiting for transfers between devices, body(): lax.all_gather(mixing_grad, 'resp', axis=0, tiled=True)  49.1 us
    all_gather x1, blocking collectives, body(): lax.all_gather(prompt_keys, 'resp', axis=0, tiled=True)  34.9 us
    all_gather x1, blocking collectives, body(): lax.all_gather(dkr_low, 'resp', axis=0, tiled=True)  34.7 us
    all_gather x1, blocking collectives, body(): lax.all_gather(dvp_low, 'resp', axis=0, tiled=True)  33.2 us
  transfers between devices with their start and end apart: 12, of which 12 were waited for; matrix products, arithmetic and copies ran while one was open for 8% of the time, Pallas kernels for 0%

commit v1 on v0

v1 whole, which is shorter than its diff:
```python
import math

import jax
import jax.numpy as jnp
from jax import lax
from jax.sharding import PartitionSpec as P

HD = 128


norm_eps = 1e-06
rope_base = 1000000.0
clip_low = 0.8
clip_high = 1.28
kl_weight = 0.04


def norm_rope(values, scale_gain, positions):
    row_count = values.shape[0]
    head_count = values.shape[1] // HD
    shaped = values.reshape(row_count, head_count, HD)
    mean_square = jnp.mean(shaped * shaped, axis=-1, keepdims=True)
    normed = shaped * lax.rsqrt(mean_square + norm_eps) * scale_gain
    half_dim = HD // 2
    frequency = jnp.exp(jnp.arange(half_dim, dtype=jnp.float32) * (-2.0 * math.log(rope_base) / HD))
    angles = positions[:, None] * frequency[None, :]
    cosine_table = jnp.cos(angles)[:, None, :]
    sine_table = jnp.sin(angles)[:, None, :]
    first_half = normed[..., :half_dim]
    second_half = normed[..., half_dim:]
    rotated = jnp.concatenate(
        [
            first_half * cosine_table - second_half * sine_table,
            second_half * cosine_table + first_half * sine_table,
        ],
        axis=-1,
    )
    return rotated.reshape(row_count, head_count * HD)


def rope_back(pre_values, scale_gain, positions, cotangent):
    result = jax.vjp(
        lambda inner_values: norm_rope(inner_values, scale_gain, positions), pre_values
    )[1](cotangent)
    return result[0]


def seen_mask(query_count, key_count, prompt_count):
    query_index = jnp.arange(query_count)[:, None]
    key_index = jnp.arange(key_count)[None, :]
    return (key_index < prompt_count) | (key_index - prompt_count <= query_index)


def split_heads(query, keys, values):
    row_count = query.shape[0]
    key_count = keys.shape[0]
    kv_heads = keys.shape[1] // HD
    group_size = query.shape[1] // keys.shape[1]
    query_heads = query.reshape(row_count, kv_heads, group_size, HD)
    key_heads = keys.reshape(key_count, kv_heads, HD)
    value_heads = values.reshape(key_count, kv_heads, HD)
    return (query_heads, key_heads, value_heads)


def attend(query, keys, values, prompt_count):
    query_heads, key_heads, value_heads = split_heads(query, keys, values)
    row_count = query.shape[0]
    scores = jnp.einsum(
        "tkgh,nkh->kgtn", query_heads, key_heads, preferred_element_type=jnp.float32
    ) * HD ** (-0.5)
    weights = jnp.where(seen_mask(row_count, keys.shape[0], prompt_count), jnp.exp(scores), 0.0)
    probs = weights / jnp.sum(weights, axis=-1, keepdims=True)
    probs_low = probs.astype(jnp.bfloat16)
    mixed = jnp.einsum("kgtn,nkh->tkgh", probs_low, value_heads, preferred_element_type=jnp.float32)
    return (mixed.reshape(row_count, -1).astype(jnp.bfloat16), probs, probs_low)


def attend_back(query, keys, values, probs, probs_low, grad_low):
    query_heads, key_heads, value_heads = split_heads(query, keys, values)
    row_count = query.shape[0]
    key_count = keys.shape[0]
    grad_heads = grad_low.reshape(query_heads.shape)
    value_cot = jnp.einsum(
        "kgtn,tkgh->nkh", probs_low, grad_heads, preferred_element_type=jnp.float32
    )
    prob_cot = jnp.einsum(
        "tkgh,nkh->kgtn", grad_heads, value_heads, preferred_element_type=jnp.float32
    )
    inner_sum = jnp.sum(probs * prob_cot, axis=-1, keepdims=True)
    score_cot = (probs * (prob_cot - inner_sum) * HD ** (-0.5)).astype(jnp.bfloat16)
    query_cot = jnp.einsum(
        "kgtn,nkh->tkgh", score_cot, key_heads, preferred_element_type=jnp.float32
    ).reshape(row_count, -1)
    key_cot = jnp.einsum(
        "kgtn,tkgh->nkh", score_cot, query_heads, preferred_element_type=jnp.float32
    ).reshape(key_count, -1)
    return (query_cot, key_cot, value_cot.reshape(key_count, -1))


def objective(logprob, behavior, reference_lp, advantage, live):
    ratios = jnp.exp(logprob - behavior)
    weight = jnp.clip(ratios, clip_low, clip_high)
    ref_gap = reference_lp - logprob
    penalty = jnp.exp(ref_gap) - ref_gap - 1.0
    token_loss = live * (kl_weight * penalty - weight * advantage * logprob)
    lp_slope = live * (kl_weight * (1.0 - jnp.exp(ref_gap)) - weight * advantage)
    return (jnp.sum(token_loss), lp_slope)


def swap_sum(value, axis):
    size = lax.axis_size(axis)
    step = 1
    while step < size:
        value = value + lax.ppermute(value, axis, [(i, i ^ step) for i in range(size)])
        step *= 2
    return value


def exchange(blocks):
    return lax.all_to_all(blocks, "resp", split_axis=0, concat_axis=0, tiled=True)


def spread(block, groups):
    return exchange(jnp.broadcast_to(block[None], (groups,) + block.shape))


def body(
    resp_hidden,
    prompt_hidden,
    readout,
    query_weight,
    key_weight,
    value_weight,
    out_weight,
    query_gain,
    key_gain,
    base_logprob,
    behavior_logprob,
    reference_logprob,
    rewards,
    lengths,
):
    own_x = resp_hidden[0]
    own_read = readout[0]
    rows = own_x.shape[0]
    qcols = query_weight.shape[1]
    kcols = key_weight.shape[1]
    groups = lax.axis_size("resp")
    index = lax.axis_index("resp")
    width = own_x.shape[1] // groups
    bf16 = jnp.bfloat16

    reward_sum = swap_sum(rewards, "resp")[0]
    tokens = jnp.concatenate([own_x, prompt_hidden, own_read], axis=0)
    tokens = exchange(tokens.reshape(3 * rows, groups, width).transpose(1, 0, 2))
    cols_x = tokens[:, :rows]
    cols_p = tokens[:, rows : 2 * rows]
    cols_r = tokens[:, 2 * rows :]

    def project(left, right):
        return jnp.einsum("ntd,dc->ntc", left, right, preferred_element_type=jnp.float32).astype(bf16)

    partial_terms = jnp.concatenate(
        [
            project(cols_x, query_weight),
            project(cols_r, out_weight),
            project(cols_x, key_weight),
            project(cols_x, value_weight),
            project(cols_p, key_weight),
            project(cols_p, value_weight),
        ],
        axis=2,
    )
    sums = jnp.sum(exchange(partial_terms).astype(jnp.float32), axis=0)
    q_pre = sums[:, :qcols]
    mixing = sums[:, qcols : 2 * qcols]
    kr_pre, vr_pre, kp_pre, vp_pre = (
        sums[:, 2 * qcols + n * kcols : 2 * qcols + (n + 1) * kcols] for n in range(4)
    )
    prompt_pos = (index * rows + jnp.arange(rows)).astype(jnp.float32)
    resp_pos = (rows * groups + jnp.arange(rows)).astype(jnp.float32)
    prompt_keys = norm_rope(kp_pre, key_gain, prompt_pos).astype(bf16)
    prompt_kv = spread(jnp.concatenate([prompt_keys, vp_pre.astype(bf16)], axis=1), groups)
    prompt_count = rows * groups
    prompt_kv = prompt_kv.reshape(prompt_count, 2 * kcols)
    query = norm_rope(q_pre, query_gain, resp_pos).astype(bf16)
    resp_keys = norm_rope(kr_pre, key_gain, resp_pos).astype(bf16)
    keys = jnp.concatenate([prompt_kv[:, :kcols], resp_keys], axis=0)
    values = jnp.concatenate([prompt_kv[:, kcols:], vr_pre.astype(bf16)], axis=0)
    mixed, probs, probs_low = attend(query, keys, values, prompt_count)
    mixed_wide = mixed.astype(jnp.float32)
    attn_part = jnp.sum(mixed_wide * mixing, axis=-1)
    own_part = jnp.einsum("td,td->t", own_x, own_read, preferred_element_type=jnp.float32)
    attn_logit = swap_sum(attn_part[None, :], "head")[0]
    logprob = base_logprob[0] + own_part + attn_logit
    advantage = rewards[0] - reward_sum / groups
    live = (jnp.arange(rows) < lengths[0]).astype(jnp.float32)
    loss_own, lp_slope = objective(
        logprob, behavior_logprob[0], reference_logprob[0], advantage, live
    )
    group_loss = swap_sum(loss_own.reshape(1), "resp")
    mixed_grad = (lp_slope[:, None] * mixing).astype(bf16)
    mixing_grad = (lp_slope[:, None] * mixed_wide).astype(bf16)
    query_cot, key_cot, value_cot = attend_back(query, keys, values, probs, probs_low, mixed_grad)
    prompt_cots = jnp.concatenate(
        [key_cot[:prompt_count].astype(bf16), value_cot[:prompt_count].astype(bf16)], axis=1
    )
    prompt_cots = jnp.sum(
        exchange(prompt_cots.reshape(groups, rows, 2 * kcols)).astype(jnp.float32), axis=0
    )
    dkp_low = rope_back(kp_pre, key_gain, prompt_pos, prompt_cots[:, :kcols]).astype(bf16)
    dvp_low = prompt_cots[:, kcols:].astype(bf16)
    dq_low = rope_back(q_pre, query_gain, resp_pos, query_cot).astype(bf16)
    dkr_low = rope_back(kr_pre, key_gain, resp_pos, key_cot[prompt_count:]).astype(bf16)
    dvr_low = value_cot[prompt_count:].astype(bf16)
    cots = spread(
        jnp.concatenate([dq_low, mixing_grad, dkr_low, dvr_low, dkp_low, dvp_low], axis=1), groups
    )

    def weight_grad(left, right):
        return jnp.einsum("ntd,ntc->dc", left, right, preferred_element_type=jnp.float32)

    kv_grad = weight_grad(cols_x, cots[:, :, 2 * qcols : 2 * qcols + 2 * kcols]) + weight_grad(
        cols_p, cots[:, :, 2 * qcols + 2 * kcols :]
    )
    return (
        logprob[None, :],
        group_loss,
        weight_grad(cols_x, cots[:, :, :qcols]).astype(bf16),
        kv_grad[:, :kcols].astype(bf16),
        kv_grad[:, kcols:].astype(bf16),
        weight_grad(cols_r, cots[:, :, qcols : 2 * qcols]).astype(bf16),
    )


def solution(mesh):
    placed = (
        P(("grp", "resp"), None, None),
        P(("grp", "resp"), None),
        P(("grp", "resp"), None, None),
        P("resp", "head"),
        P("resp", "head"),
        P("resp", "head"),
        P("resp", "head"),
        P(),
        P(),
        P(("grp", "resp"), None),
        P(("grp", "resp"), None),
        P(("grp", "resp"), None),
        P(("grp", "resp")),
        P(("grp", "resp")),
    )
    return jax.shard_map(
        body,
        mesh=mesh,
        in_specs=placed,
        out_specs=(
            P(("grp", "resp"), None),
            P("grp"),
            P(("grp", "resp"), "head"),
            P(("grp", "resp"), "head"),
            P(("grp", "resp"), "head"),
            P(("grp", "resp"), "head"),
        ),
        check_vma=False,
    )
```

time: 919 us -> 339 us (0.37)
  waiting for transfers between devices: 460 us -> 130 us
  blocking collectives: 281 us -> 53.8 us
  starting transfers between devices: 13.4 us -> 56.5 us
  other arithmetic: 55.5 us -> 27.1 us
  matrix products: 49.6 us -> 34 us
  local copies, waits for them, and re-layouts: 40.4 us -> 26.5 us
    reduce_scatter x8 -> x0, waiting for transfers between devices: 356 us -> none  [the longest x1 78.4 us: body(): lax.psum_scatter(partial_terms[2], 'resp', scatter_dimension=0, tiled=True)]
    all_gather x6 -> x0, blocking collectives: 200 us -> none  [the longest x1 34.9 us: body(): lax.all_gather(prompt_keys, 'resp', axis=0, tiled=True)]
    all_gather x2 -> x0, waiting for transfers between devices: 76.5 us -> none  [the longest x1 49.1 us: body(): lax.all_gather(mixing_grad, 'resp', axis=0, tiled=True)]
    psum x3 -> x0, blocking collectives: 57.8 us -> none  [the longest x1 20.3 us: body(): reward_sum = lax.psum(rewards, 'resp')[0]]
    ppermute x0 -> x9, waiting for transfers between devices: none -> 51.7 us  [swap_sum(): lax.ppermute(value, axis, [(i, i ^ step) for i in range(size)])]
    all_to_all x2 -> x4, waiting for transfers between devices: 27.1 us -> 78.2 us  [exchange(): lax.all_to_all(blocks, 'resp', split_axis=0, concat_axis=0, tiled=True)]
    ppermute x0 -> x9, starting transfers between devices: none -> 31.9 us  [swap_sum(): lax.ppermute(value, axis, [(i, i ^ step) for i in range(size)])]
    all_to_all x1, blocking collectives: 23.1 us -> 53.8 us  [exchange(): lax.all_to_all(blocks, 'resp', split_axis=0, concat_axis=0, tiled=True)]
  transfers between devices with their start and end apart: 12 -> 13, of which waited for: 12 -> 8; matrix products, arithmetic and copies ran while one was open for 8% -> 4% of each run, Pallas kernels for 0% -> 0%
where the time goes in v1:
time: 339 us; the launch traced here: 336 us
  waiting for transfers between devices  130 us (38%)
  starting transfers between devices  56.5 us (17%)
  blocking collectives  53.8 us (16%)
  matrix products  34 us (10%)
  other arithmetic  27.1 us (8%)
  local copies, waits for them, and re-layouts  26.5 us (8%)
  between operations  8.28 us (2%)
    all_to_all x4, waiting for transfers between devices, exchange(): lax.all_to_all(blocks, 'resp', split_axis=0, concat_axis=0, tiled=True)  78.2 us
    all_to_all x1, blocking collectives, exchange(): lax.all_to_all(blocks, 'resp', split_axis=0, concat_axis=0, tiled=True)  53.8 us
    ppermute x9, waiting for transfers between devices, swap_sum(): lax.ppermute(value, axis, [(i, i ^ step) for i in range(size)])  51.7 us
    ppermute x9, starting transfers between devices, swap_sum(): lax.ppermute(value, axis, [(i, i ^ step) for i in range(size)])  31.9 us
    all_to_all x4, starting transfers between devices, exchange(): lax.all_to_all(blocks, 'resp', split_axis=0, concat_axis=0, tiled=True)  24.6 us
    dot_general x4, matrix products, weight_grad(): jnp.einsum('ntd,ntc->dc', left, right, preferred_element_type=jnp.float32)  12.7 us
    dot_general x6, matrix products, project(): jnp.einsum('ntd,dc->ntc', left, right, preferred_element_type=jnp.float32)  11.5 us
    unnamed x84, local copies, waits for them, and re-layouts  9.79 us
  transfers between devices with their start and end apart: 13, of which 8 were waited for; matrix products, arithmetic and copies ran while one was open for 4% of the time, Pallas kernels for 0%

profile of v1, /device:TPU:2, one launch (start us, length us, event | category | flops | bytes accessed | tf_op | source)
XLA Modules:
  0.0 336.1 jit_solution(15991394687484795138)
XLA Ops:
  15.6 53.8 %all_to_all.25 = bf16[8,384,640]{2,1,0:T(8,128)(2,1)S(1)} all-to-all(bf16[8,384,640]{2,1,0:T(8,128)(2,1)S(1)} %maximum_bitcast_fusion), channel_id=1, replica_groups=mesh['grp'=4,'resp'=8,'head'=8] {'resp'}, dimensions={0} | all-to-all | bytes 7864320 | tf_op jit(solution)/shard_map/all_to_all | solution.py:120
  69.4 3.3 convert_dynamic-update-slice_fusion.1
  72.7 3.2 convert_dynamic-update-slice_fusion
  80.9 5.9 %all-to-all-start.1 = ((bf16[8,128,2560]{2,1,0:T(8,128)(2,1)}), bf16[8,128,2560]{2,1,0:T(8,128)(2,1)}, u32[]{:S(2)}, u32[]{:S(2)}) async-start(bf16[8,128,2560]{2,1,0:T(8,128)(2,1)} %fusion.20), calls=%async_computation.1 | async-start | bytes 10485760 | tf_op jit(solution)/shard_map/all_to_all | solution.py:120
  89.9 65.4 %all-to-all-done.1 = bf16[8,128,2560]{2,1,0:T(8,128)(2,1)} async-done(((bf16[8,128,2560]{2,1,0:T(8,128)(2,1)}), bf16[8,128,2560]{2,1,0:T(8,128)(2,1)}, u32[]{:S(2)}, u32[]{:S(2)}) %all-to-all-start.1) | async-done | bytes 5242912 | tf_op jit(solution)/shard_map/all_to_all | solution.py:120
  155.2 3.3 convert_reduce_fusion
  164.2 7.2 %all-to-all-start.2 = ((bf16[8,128,256]{2,1,0:T(8,128)(2,1)}), bf16[8,128,256]{2,1,0:T(8,128)(2,1)S(1)}, u32[]{:S(2)}, u32[]{:S(2)}) async-start(bf16[8,128,256]{2,1,0:T(8,128)(2,1)} %broadcast_in_dim.20), calls=%async_computation.2 | async-start | bytes 1048576 | tf_op jit(solution)/shard_map/all_to_all | solution.py:120
  173.4 6.2 %all-to-all-done.2 = bf16[8,128,256]{2,1,0:T(8,128)(2,1)S(1)} async-done(((bf16[8,128,256]{2,1,0:T(8,128)(2,1)}), bf16[8,128,256]{2,1,0:T(8,128)(2,1)S(1)}, u32[]{:S(2)}, u32[]{:S(2)}) %all-to-all-start.2) | async-done | bytes 524320 | tf_op jit(solution)/shard_map/all_to_all | solution.py:120
  192.0 3.3 collective-permute-start.1
  199.4 5.5 %collective-permute-start.2 = (f32[1,128]{1,0:T(1,128)S(1)}, f32[1,128]{1,0:T(1,128)S(1)}, u32[]{:S(2)}, u32[]{:S(2)}) collective-permute-start(f32[1,128]{1,0:T(1,128)S(1)} %add.161), channel_id=1, source_target_pairs={{0,4},{1,5},{2,6},{3,7},{4,0},{5,1},{6,2},{7,3},{8,12},{9,13},{10,... | collective-permute-start | bytes 1544 | tf_op jit(solution)/shard_map/ppermute | solution.py:114
  204.9 2.7 collective-permute-start.4
  209.2 3.0 collective-permute-start.5
  215.1 2.9 copy.103
  219.4 3.3 fusion
  227.8 5.5 %all-to-all-start.3 = ((bf16[8,128,256]{2,1,0:T(8,128)(2,1)}), bf16[8,128,256]{2,1,0:T(8,128)(2,1)}, u32[]{:S(2)}, u32[]{:S(2)}) async-start(bf16[8,128,256]{2,1,0:T(8,128)(2,1)} %pad_maximum_fusion), calls=%async_computation.3 | async-start | bytes 1048576 | tf_op jit(solution)/shard_map/all_to_all | solution.py:120
  235.0 6.6 %all-to-all-done.3 = bf16[8,128,256]{2,1,0:T(8,128)(2,1)} async-done(((bf16[8,128,256]{2,1,0:T(8,128)(2,1)}), bf16[8,128,256]{2,1,0:T(8,128)(2,1)}, u32[]{:S(2)}, u32[]{:S(2)}) %all-to-all-start.3) | async-done | bytes 524320 | tf_op jit(solution)/shard_map/all_to_all | solution.py:120
  247.2 2.8 broadcast_in_dim.30
  250.1 6.0 %all-to-all-start.4 = ((bf16[8,128,2560]{2,1,0:T(8,128)(2,1)}), bf16[8,128,2560]{2,1,0:T(8,128)(2,1)}, u32[]{:S(2)}, u32[]{:S(2)}) async-start(bf16[8,128,2560]{2,1,0:T(8,128)(2,1)} %broadcast_in_dim.30), calls=%async_computation.4 | async-start | bytes 10485760 | tf_op jit(solution)/shard_map/all_to_all | solution.py:120
  256.7 3.0 collective-permute-start.6
  259.7 48.0 %collective-permute-done.6 = f32[1]{0:T(128)} collective-permute-done((f32[1]{0:T(128)}, f32[1]{0:T(128)}, u32[]{:S(2)}, u32[]{:S(2)}) %collective-permute-start.6) | collective-permute-done | bytes 36 | tf_op jit(solution)/shard_map/ppermute | solution.py:114
  308.9 4.8 %collective-permute-start.7 = (f32[1]{0:T(128)}, f32[1]{0:T(128)}, u32[]{:S(2)}, u32[]{:S(2)}) collective-permute-start(f32[1]{0:T(128)} %add.167), channel_id=1, source_target_pairs={{0,16},{8,24},{16,0},{24,8},{32,48},{40,56},{48,32},{56,40},{1,17}... | collective-permute-start | bytes 20 | tf_op jit(solution)/shard_map/ppermute | solution.py:114
  314.4 6.3 %collective-permute-start.8 = (f32[1]{0:T(128)}, f32[1]{0:T(128)}, u32[]{:S(2)}, u32[]{:S(2)}) collective-permute-start(f32[1]{0:T(128)} %add.168), channel_id=1, source_target_pairs={{0,32},{8,40},{16,48},{24,56},{32,0},{40,8},{48,16},{56,24},{1,33}... | collective-permute-start | bytes 20 | tf_op jit(solution)/shard_map/ppermute | solution.py:114
  326.4 4.3 %bitcast_convert_fusion = bf16[640,1024]{1,0:T(8,128)(2,1)} fusion(bf16[8,128,2560]{2,1,0:T(8,128)(2,1)} %all-to-all-done.4, bf16[8,384,640]{2,1,0:T(8,128)(2,1)S(1)} %copy-done.7), kind=kOutput, calls=%fused_computation.10 | convolution fusion | flops 1342832640 | bytes 4718592 | tf_op jit(solution)/shard_map/ntd,ntc->dc/dot_general | solution.py:221
  330.7 4.2 %bitcast_convert_fusion.1 = bf16[640,1024]{1,0:T(8,128)(2,1)} fusion(bf16[8,128,2560]{2,1,0:T(8,128)(2,1)} %all-to-all-done.4, bf16[8,384,640]{2,1,0:T(8,128)(2,1)S(1)} %copy-done.7), kind=kOutput, calls=%fused_computation.11 | convolution fusion | flops 1342832640 | bytes 4718592 | tf_op jit(solution)/shard_map/ntd,ntc->dc/dot_general | solution.py:221
  (166 shorter events, 67.2 us)
Async XLA Ops:
  0.6 68.7 %copy-start = (bf16[640,1024]{1,0:T(8,128)(2,1)S(1)}, bf16[640,1024]{1,0:T(8,128)(2,1)}, u32[]{:S(2)}) copy-start(bf16[640,1024]{1,0:T(8,128)(2,1)} %param.17) | copy-start | bytes 3932164
  80.9 74.3 %all-to-all-start.1 = ((bf16[8,128,2560]{2,1,0:T(8,128)(2,1)}), bf16[8,128,2560]{2,1,0:T(8,128)(2,1)}, u32[]{:S(2)}, u32[]{:S(2)}) async-start(bf16[8,128,2560]{2,1,0:T(8,128)(2,1)} %fusion.20), calls=%async_computation.1 | async-start | bytes 10485760 | tf_op jit(solution)/shard_map/all_to_all | solution.py:120
  158.6 23.5 %copy-start.3 = (f32[128,2560]{1,0:T(8,128)}, f32[128,2560]{1,0:T(8,128)S(1)}, u32[]{:S(2)}) copy-start(f32[128,2560]{1,0:T(8,128)S(1)} %convert_reduce_fusion) | copy-start | bytes 3932164
  164.2 15.5 %all-to-all-start.2 = ((bf16[8,128,256]{2,1,0:T(8,128)(2,1)}), bf16[8,128,256]{2,1,0:T(8,128)(2,1)S(1)}, u32[]{:S(2)}, u32[]{:S(2)}) async-start(bf16[8,128,256]{2,1,0:T(8,128)(2,1)} %broadcast_in_dim.20), calls=%async_computation.2 | async-start | bytes 1048576 | tf_op jit(solution)/shard_map/all_to_all | solution.py:120
  173.4 11.2 %copy-start.9 = (bf16[128,8,64]{2,0,1:T(8,128)(2,1)}, bf16[128,8,64]{2,0,1:T(8,128)(2,1)S(1)}, u32[]{:S(2)}) copy-start(bf16[128,8,64]{2,0,1:T(8,128)(2,1)S(1)} %get-tuple-element.20) | copy-start | bytes 393220
  173.4 11.2 %copy-start.11 = (bf16[128,8,64]{2,0,1:T(8,128)(2,1)}, bf16[128,8,64]{2,0,1:T(8,128)(2,1)S(1)}, u32[]{:S(2)}) copy-start(bf16[128,8,64]{2,0,1:T(8,128)(2,1)S(1)} %get-tuple-element.21) | copy-start | bytes 393220
  188.4 29.6 %copy-start.30 = (f32[1,128]{1,0:T(1,128)S(1)}, f32[1,128]{1,0:T(1,128)}, u32[]{:S(2)}) copy-start(f32[1,128]{1,0:T(1,128)} %param.25) | copy-start | bytes 1540
  188.4 29.6 %copy-start.31 = (f32[1,128]{1,0:T(1,128)S(1)}, f32[1,128]{1,0:T(1,128)}, u32[]{:S(2)}) copy-start(f32[1,128]{1,0:T(1,128)} %param.24) | copy-start | bytes 1540
  188.4 29.6 %copy-start.33 = (f32[1,128]{1,0:T(1,128)S(1)}, f32[1,128]{1,0:T(1,128)}, u32[]{:S(2)}) copy-start(f32[1,128]{1,0:T(1,128)} %param.23) | copy-start | bytes 1540
  188.4 3.6 %collective-permute-start = (f32[1,128]{1,0:T(1,128)S(1)}, f32[1,128]{1,0:T(1,128)S(1)}, u32[]{:S(2)}, u32[]{:S(2)}) collective-permute-start(f32[1,128]{1,0:T(1,128)S(1)} %bitcast.215), channel_id=1, source_target_pairs={{0,1},{1,0},{2,3},{3,2},{4,5},{5,4},{6,7},{7,6},{8,9},{9,8},{10,11... | collective-permute-start | bytes 1544 | tf_op jit(solution)/shard_map/ppermute | solution.py:114
  190.4 8.4 %collective-permute-start.3 = (f32[1]{0:T(128)}, f32[1]{0:T(128)}, u32[]{:S(2)}, u32[]{:S(2)}) collective-permute-start(f32[1]{0:T(128)} %param.26), channel_id=1, source_target_pairs={{0,8},{8,0},{16,24},{24,16},{32,40},{40,32},{48,56},{56,48},{1,9},... | collective-permute-start | bytes 20 | tf_op jit(solution)/shard_map/ppermute | solution.py:114
  192.0 7.4 %collective-permute-start.1 = (f32[1,128]{1,0:T(1,128)S(1)}, f32[1,128]{1,0:T(1,128)S(1)}, u32[]{:S(2)}, u32[]{:S(2)}) collective-permute-start(f32[1,128]{1,0:T(1,128)S(1)} %bitcast_add_fusion.2), channel_id=1, source_target_pairs={{0,2},{1,3},{2,0},{3,1},{4,6},{5,7},{6,4},{7,5},{8,10},{9,11},{10,... | collective-permute-start | bytes 1544 | tf_op jit(solution)/shard_map/ppermute | solution.py:114
  199.4 18.6 %collective-permute-start.2 = (f32[1,128]{1,0:T(1,128)S(1)}, f32[1,128]{1,0:T(1,128)S(1)}, u32[]{:S(2)}, u32[]{:S(2)}) collective-permute-start(f32[1,128]{1,0:T(1,128)S(1)} %add.161), channel_id=1, source_target_pairs={{0,4},{1,5},{2,6},{3,7},{4,0},{5,1},{6,2},{7,3},{8,12},{9,13},{10,... | collective-permute-start | bytes 1544 | tf_op jit(solution)/shard_map/ppermute | solution.py:114
  204.9 3.6 %collective-permute-start.4 = (f32[1]{0:T(128)}, f32[1]{0:T(128)}, u32[]{:S(2)}, u32[]{:S(2)}) collective-permute-start(f32[1]{0:T(128)} %add.164), channel_id=1, source_target_pairs={{0,16},{8,24},{16,0},{24,8},{32,48},{40,56},{48,32},{56,40},{1,17}... | collective-permute-start | bytes 20 | tf_op jit(solution)/shard_map/ppermute | solution.py:114
  209.2 5.2 %collective-permute-start.5 = (f32[1]{0:T(128)}, f32[1]{0:T(128)}, u32[]{:S(2)}, u32[]{:S(2)}) collective-permute-start(f32[1]{0:T(128)} %add.165), channel_id=1, source_target_pairs={{0,32},{8,40},{16,48},{24,56},{32,0},{40,8},{48,16},{56,24},{1,33}... | collective-permute-start | bytes 20 | tf_op jit(solution)/shard_map/ppermute | solution.py:114
  218.1 38.0 %copy-start.32 = (f32[128]{0:T(128)}, f32[128]{0:T(128)S(1)}, u32[]{:S(2)}) copy-start(f32[128]{0:T(128)S(1)} %get-tuple-element.11) | copy-start | bytes 1540
  227.8 13.8 %all-to-all-start.3 = ((bf16[8,128,256]{2,1,0:T(8,128)(2,1)}), bf16[8,128,256]{2,1,0:T(8,128)(2,1)}, u32[]{:S(2)}, u32[]{:S(2)}) async-start(bf16[8,128,256]{2,1,0:T(8,128)(2,1)} %pad_maximum_fusion), calls=%async_computation.3 | async-start | bytes 1048576 | tf_op jit(solution)/shard_map/all_to_all | solution.py:120
  233.6 10.8 %copy-start.27 = (f32[128]{0:T(128)S(1)}, f32[128]{0:T(128)}, u32[]{:S(2)}) copy-start(f32[128]{0:T(128)} %copy-done.26) | copy-start | bytes 1540
  233.6 10.9 %copy-start.25 = (f32[128]{0:T(128)S(1)}, f32[128]{0:T(128)}, u32[]{:S(2)}) copy-start(f32[128]{0:T(128)} %fusion.97) | copy-start | bytes 1540
  233.6 12.6 %copy-start.23 = (f32[128]{0:T(128)S(1)}, f32[128]{0:T(128)}, u32[]{:S(2)}) copy-start(f32[128]{0:T(128)} %fusion.96) | copy-start | bytes 1540
  250.1 71.5 %all-to-all-start.4 = ((bf16[8,128,2560]{2,1,0:T(8,128)(2,1)}), bf16[8,128,2560]{2,1,0:T(8,128)(2,1)}, u32[]{:S(2)}, u32[]{:S(2)}) async-start(bf16[8,128,2560]{2,1,0:T(8,128)(2,1)} %broadcast_in_dim.30), calls=%async_computation.4 | async-start | bytes 10485760 | tf_op jit(solution)/shard_map/all_to_all | solution.py:120
  256.7 51.0 %collective-permute-start.6 = (f32[1]{0:T(128)}, f32[1]{0:T(128)}, u32[]{:S(2)}, u32[]{:S(2)}) collective-permute-start(f32[1]{0:T(128)} %bitcast.34), channel_id=1, source_target_pairs={{0,8},{8,0},{16,24},{24,16},{32,40},{40,32},{48,56},{56,48},{1,9},... | collective-permute-start | bytes 20 | tf_op jit(solution)/shard_map/ppermute | solution.py:114
  308.9 4.8 %collective-permute-start.7 = (f32[1]{0:T(128)}, f32[1]{0:T(128)}, u32[]{:S(2)}, u32[]{:S(2)}) collective-permute-start(f32[1]{0:T(128)} %add.167), channel_id=1, source_target_pairs={{0,16},{8,24},{16,0},{24,8},{32,48},{40,56},{48,32},{56,40},{1,17}... | collective-permute-start | bytes 20 | tf_op jit(solution)/shard_map/ppermute | solution.py:114
  314.4 6.5 %collective-permute-start.8 = (f32[1]{0:T(128)}, f32[1]{0:T(128)}, u32[]{:S(2)}, u32[]{:S(2)}) collective-permute-start(f32[1]{0:T(128)} %add.168), channel_id=1, source_target_pairs={{0,32},{8,40},{16,48},{24,56},{32,0},{40,8},{48,16},{56,24},{1,33}... | collective-permute-start | bytes 20 | tf_op jit(solution)/shard_map/ppermute | solution.py:114
  (28 other events, 126.9 us)

commit v2 on v1

v2 whole, which is shorter than its diff:
```python
import math

import jax
import jax.numpy as jnp
from jax import lax
from jax.experimental import pallas as pl
from jax.experimental.pallas import tpu as pltpu
from jax.sharding import PartitionSpec as P

HD = 128


norm_eps = 1e-06
rope_base = 1000000.0
clip_low = 0.8
clip_high = 1.28
kl_weight = 0.04


def norm_rope(values, scale_gain, positions):
    row_count = values.shape[0]
    head_count = values.shape[1] // HD
    shaped = values.reshape(row_count, head_count, HD)
    mean_square = jnp.mean(shaped * shaped, axis=-1, keepdims=True)
    normed = shaped * lax.rsqrt(mean_square + norm_eps) * scale_gain
    half_dim = HD // 2
    frequency = jnp.exp(jnp.arange(half_dim, dtype=jnp.float32) * (-2.0 * math.log(rope_base) / HD))
    angles = positions[:, None] * frequency[None, :]
    cosine_table = jnp.cos(angles)[:, None, :]
    sine_table = jnp.sin(angles)[:, None, :]
    first_half = normed[..., :half_dim]
    second_half = normed[..., half_dim:]
    rotated = jnp.concatenate(
        [
            first_half * cosine_table - second_half * sine_table,
            second_half * cosine_table + first_half * sine_table,
        ],
        axis=-1,
    )
    return rotated.reshape(row_count, head_count * HD)


def objective(logprob, behavior, reference_lp, advantage, live):
    ratios = jnp.exp(logprob - behavior)
    weight = jnp.clip(ratios, clip_low, clip_high)
    ref_gap = reference_lp - logprob
    penalty = jnp.exp(ref_gap) - ref_gap - 1.0
    token_loss = live * (kl_weight * penalty - weight * advantage * logprob)
    lp_slope = live * (kl_weight * (1.0 - jnp.exp(ref_gap)) - weight * advantage)
    return (jnp.sum(token_loss), lp_slope)


XS = 4
BF = jnp.bfloat16
F32 = jnp.float32
NT = (((1,), (1,)), ((), ()))
TN = (((0,), (0,)), ((), ()))
PAIR = 4
params = pltpu.CompilerParams(vmem_limit_bytes=30 * 1024 * 1024)
alone = pltpu.CompilerParams(vmem_limit_bytes=60 * 1024 * 1024)


TAIL = 16


def cost(us):
    return pl.CostEstimate(flops=int(us * 1e8), bytes_accessed=1 << 18, transcendentals=0)


def wide(value):
    return value.astype(F32)


def sds(shape, dtype):
    return jax.ShapeDtypeStruct(shape, dtype)


def whole(array):
    shape = array.shape
    return pl.BlockSpec(shape, lambda *_: (0,) * len(shape))


def send(value, dx, dy=0):
    pairs = [(x * 2 + y, ((x + dx) % XS) * 2 + (y ^ dy)) for x in range(XS) for y in range(2)]
    return lax.ppermute(value, "resp", pairs)


def xor_sum(value, axis):
    def flip(term, step):
        return lax.ppermute(term, axis, [(i, i ^ step) for i in range(2 * XS)])

    quad = (value + flip(value, 1)) + (flip(value, 2) + flip(value, 3))
    return quad + flip(quad, 4)


def with_scalar(block, scalar):
    high = lax.reduce_precision(scalar, 8, 7)
    rest = scalar - high
    middle = lax.reduce_precision(rest, 8, 7)
    terms = jnp.stack([high, middle, rest - middle]).astype(BF)
    tail = jnp.zeros((TAIL, block.shape[1]), BF).at[0, :3].set(terms)
    return jnp.concatenate([block, tail], axis=0)


def scalar_of(block):
    return jnp.sum(jnp.sum(wide(block[-TAIL:]), axis=0, keepdims=True), axis=1, keepdims=True)


def exchange(blocks):
    return lax.all_to_all(blocks, "resp", split_axis=0, concat_axis=0, tiled=True)


def pack(own_x, own_p, own_r):
    rows, depth = own_x.shape
    width = depth // (2 * XS)

    def kernel(x_ref, p_ref, r_ref, out_ref, acc_ref):
        x, r = x_ref[...], r_ref[...]
        for n in range(2):
            at = slice(n * width, (n + 1) * width)
            out_ref[n, :rows] = x[:, at]
            out_ref[n, rows : 2 * rows] = p_ref[:, at]
            out_ref[n, 2 * rows :] = r[:, at]
        terms = wide(x) * wide(r)
        total = sum(terms[:, n : n + HD] for n in range(0, 2 * width, HD))

        @pl.when(pl.program_id(0) == 0)
        def _():
            acc_ref[...] = total

        @pl.when(pl.program_id(0) > 0)
        def _():
            acc_ref[...] += total

    return pl.pallas_call(
        kernel,
        grid=(XS,),
        out_shape=[sds((2 * XS, 3 * rows, width), BF), sds((rows, HD), F32)],
        in_specs=[pl.BlockSpec((rows, 2 * width), lambda n: (0, n))] * 3,
        out_specs=[
            pl.BlockSpec((2, 3 * rows, width), lambda n: (n, 0, 0)),
            pl.BlockSpec((rows, HD), lambda n: (0, 0)),
        ],
        compiler_params=alone,
        cost_estimate=cost(4),
    )(own_x, own_p, own_r)


def project(order, tokens, parts, weight, by_x):
    width = tokens.shape[2]
    rows = tokens.shape[1] // 3
    cols, tile = weight.shape[1], 256
    count = XS if by_x else 2
    inner = 2 * XS // count
    kinds = sorted(set(parts))
    total = 2 * XS * len(kinds)

    def kernel(order_ref, *refs):
        blocks, weight_ref, outs, lefts = refs[:total], refs[total], refs[total + 1 : -1], refs[-1]
        for n in range(total):
            lefts[n * rows : (n + 1) * rows] = blocks[n][0]
        for c in range(cols // tile):
            at = slice(c * tile, (c + 1) * tile)
            kind = kinds.index(parts[c])
            left = lefts[kind * 2 * XS * rows : (kind + 1) * 2 * XS * rows]
            got = jnp.dot(left, weight_ref[:, at], preferred_element_type=F32).astype(BF)
            for n in range(2 * XS):
                piece = got[n * rows : (n + 1) * rows]
                if by_x:
                    outs[n % XS][n // XS, :, at] = piece
                else:
                    outs[n // XS][n % XS, :, at] = piece

    def block(part, n):
        return pl.BlockSpec((1, rows, width), lambda c, o: (o[n], part, 0))

    return pl.pallas_call(
        kernel,
        grid_spec=pltpu.PrefetchScalarGridSpec(
            num_scalar_prefetch=1,
            grid=(1,),
            in_specs=[block(part, n) for part in kinds for n in range(2 * XS)] + [whole(weight)],
            out_specs=[pl.BlockSpec((inner, rows, cols), lambda c, o: (0, 0, 0))] * count,
            scratch_shapes=[pltpu.VMEM((total * rows, width), BF)],
        ),
        out_shape=[sds((inner, rows, cols), BF)] * count,
        compiler_params=alone,
        cost_estimate=cost(4),
    )(order, *[tokens] * total, weight)


def flip_tokens(order, tokens):
    width = tokens.shape[2]
    rows = tokens.shape[1] // 3

    def kernel(order_ref, tokens_ref, x_ref, p_ref, r_ref):
        x_ref[...] = tokens_ref[0, :rows].T
        p_ref[...] = tokens_ref[0, rows : 2 * rows].T
        r_ref[...] = tokens_ref[0, 2 * rows :].T

    by_offset = pl.BlockSpec((width, rows), lambda s, o: (0, s))
    return pl.pallas_call(
        kernel,
        grid_spec=pltpu.PrefetchScalarGridSpec(
            num_scalar_prefetch=1,
            grid=(2 * XS,),
            in_specs=[pl.BlockSpec((1, 3 * rows, width), lambda s, o: (o[s], 0, 0))],
            out_specs=[by_offset] * 3,
        ),
        out_shape=[sds((width, 2 * XS * rows), BF)] * 3,
        compiler_params=params,
        cost_estimate=cost(8),
    )(order, tokens)


KV_BLOCKS = 2 * XS + 1


def kv_specs(prompt, own_kv):
    rows = own_kv.shape[0] + TAIL
    specs = [pl.BlockSpec((rows, 2 * HD), lambda h: (0, 0))] * 2
    arrays = list(prompt[:2])
    for array in prompt[2:]:
        for n in range(2):
            specs.append(pl.BlockSpec((1, rows, 2 * HD), lambda h, n=n: (n, 0, 0)))
            arrays.append(array)
    return specs + [whole(own_kv)], arrays + [own_kv]


def load_kv(refs, keys, values):
    rows = refs[-1].shape[0]
    for n, ref in enumerate(refs):
        block = ref[...].reshape(-1, 2 * HD)[:rows]
        keys[n * rows : (n + 1) * rows] = block[:, :HD]
        values[n * rows : (n + 1) * rows] = block[:, HD:]


def probabilities(query, keys, rows):
    scores = lax.dot_general(keys, query, NT, preferred_element_type=F32) * HD ** (-0.5)
    weights = jnp.exp(scores)
    key = lax.broadcasted_iota(jnp.int32, (rows, query.shape[0]), 0)
    position = lax.broadcasted_iota(jnp.int32, (rows, query.shape[0]), 1) % rows
    count = keys.shape[0] - rows
    own = jnp.where(key <= position, weights[count:], 0.0)
    weights = jnp.concatenate([weights[:count], own], axis=0)
    return weights * (1.0 / jnp.sum(weights, axis=0, keepdims=True))


def stack_heads(value):
    return jnp.concatenate([value[:, n * HD : (n + 1) * HD] for n in range(PAIR)], axis=0)


def lay_heads(value):
    rows = value.shape[0] // PAIR
    return jnp.concatenate([value[n * rows : (n + 1) * rows] for n in range(PAIR)], axis=1)


def turn(normed, cosine, sine):
    return normed * cosine + pltpu.roll(normed, HD // 2, 1) * sine


def turn_back(pre, gain, cosine, sine, cotangent):
    scale = lax.rsqrt(jnp.mean(pre * pre, axis=-1, keepdims=True) + norm_eps)
    half = HD // 2
    flipped = jnp.concatenate([cotangent[:, half:], cotangent[:, :half]], axis=1)
    inner = (cotangent * cosine - flipped * sine) * gain
    return scale * inner - pre * (scale * scale * scale * jnp.mean(pre * inner, axis=-1, keepdims=True))


def attention(q_first, q_rest, m_pairs, m_last, prompt, own_kv, cosine, sine, gain):
    rows, cols = m_last.shape[0], m_last.shape[1] - 2 * HD
    wide_cols = PAIR * HD
    count = KV_BLOCKS * rows
    specs, arrays = kv_specs(prompt, own_kv)
    stacked = pl.BlockSpec((1, rows, wide_cols), lambda h: (0, 0, h))
    flat = pl.BlockSpec((rows, wide_cols), lambda h: (0, h))

    def kernel(*refs):
        q_in, m_in, rest = refs[:5], refs[5:10], refs[10:]
        kv_in, rest = rest[:KV_BLOCKS], rest[KV_BLOCKS:]
        cos_ref, sin_ref, gain_ref = rest[:3]
        pre_ref, query_ref, mixed_ref, mixing_ref, acc_ref, sum_ref = rest[3:9]
        keys, values, flipped = rest[9:]

        @pl.when(pl.program_id(0) == 0)
        def _():
            acc_ref[...] = jnp.zeros_like(acc_ref)
            load_kv(kv_in, keys, values)
            flipped[...] = values[...].T
            total = sum(scalar_of(r[...].reshape(-1, 2 * HD)) for r in kv_in[:-1])
            sum_ref[...] = jnp.broadcast_to(total, sum_ref.shape)

        pre = sum(wide(r[0]) for r in q_in[:2]) + sum(wide(r[...]) for r in q_in[2:])
        mixing = sum(wide(r[0]) for r in m_in[:4]) + wide(m_in[4][...])
        stack = stack_heads(pre)
        pre_ref[...] = stack
        mixing_ref[...] = stack_heads(mixing)
        scale = lax.rsqrt(jnp.mean(stack * stack, axis=-1, keepdims=True) + norm_eps)
        cosine = jnp.concatenate([cos_ref[...]] * PAIR, axis=0)
        sine = jnp.concatenate([sin_ref[...]] * PAIR, axis=0)
        query = turn(stack * scale * gain_ref[...], cosine, sine).astype(BF)
        probs = probabilities(query, keys[...], rows)
        mixed = jnp.dot(flipped[...], probs.astype(BF), preferred_element_type=F32)
        mixed = lay_heads(mixed.T).astype(BF)
        query_ref[...] = query
        mixed_ref[...] = mixed
        terms = wide(mixed) * mixing
        acc_ref[...] += sum(terms[:, n * HD : (n + 1) * HD] for n in range(PAIR))

    heads = cols // HD
    wide_out = sds((heads * rows, HD), F32)
    low_out = sds((heads * rows, HD), BF)
    tall = pl.BlockSpec((PAIR * rows, HD), lambda h: (h, 0))
    return pl.pallas_call(
        kernel,
        grid=(cols // wide_cols,),
        in_specs=[stacked] * 2 + [flat] * 3 + [stacked] * 4 + [flat]
        + specs
        + [whole(v) for v in (cosine, sine, gain)],
        out_specs=[tall, tall, flat, tall]
        + [pl.BlockSpec((rows, HD), lambda h: (0, 0)), pl.BlockSpec((8, HD), lambda h: (0, 0))],
        out_shape=[wide_out, low_out, sds((rows, cols), BF), wide_out]
        + [sds((rows, HD), F32), sds((8, HD), F32)],
        scratch_shapes=[
            pltpu.VMEM((count, HD), BF),
            pltpu.VMEM((count, HD), BF),
            pltpu.VMEM((HD, count), BF),
        ],
        compiler_params=alone,
        cost_estimate=cost(8),
    )(*q_first, *q_rest, *m_pairs, m_last, *arrays, cosine, sine, gain)


def attention_slopes(pre, query, mixing, prompt, own_kv, cosine, sine, gain):
    rows = own_kv.shape[0]
    cols = query.shape[0] // rows * HD
    wide_cols = PAIR * HD
    count = KV_BLOCKS * rows
    tall = pl.BlockSpec((PAIR * rows, HD), lambda h: (h, 0))
    across = pl.BlockSpec((count, PAIR * rows), lambda h: (0, h))
    specs, arrays = kv_specs(prompt, own_kv)

    def kernel(pre_ref, query_ref, mixing_ref, *refs):
        kv_in, rest = refs[:KV_BLOCKS], refs[KV_BLOCKS:]
        cos_ref, sin_ref, gain_ref, probs_ref, score_ref, back_ref, keys, values, flipped = rest

        @pl.when(pl.program_id(0) == 0)
        def _():
            load_kv(kv_in, keys, values)
            flipped[...] = keys[...].T

        query = query_ref[...]
        probs = probabilities(query, keys[...], rows)
        probs_ref[...] = probs.astype(BF)
        grad = mixing_ref[...].astype(BF)
        prob_cot = lax.dot_general(values[...], grad, NT, preferred_element_type=F32)
        inner = jnp.sum(probs * prob_cot, axis=0, keepdims=True)
        score_cot = (probs * (prob_cot - inner) * HD ** (-0.5)).astype(BF)
        score_ref[...] = score_cot
        query_cot = jnp.dot(flipped[...], score_cot, preferred_element_type=F32).T
        cosine = jnp.concatenate([cos_ref[...]] * PAIR, axis=0)
        sine = jnp.concatenate([sin_ref[...]] * PAIR, axis=0)
        back_ref[...] = lay_heads(
            turn_back(pre_ref[...], gain_ref[...], cosine, sine, query_cot)
        )

    return pl.pallas_call(
        kernel,
        grid=(cols // wide_cols,),
        in_specs=[tall] * 3 + specs + [whole(v) for v in (cosine, sine, gain)],
        out_specs=[across, across, pl.BlockSpec((rows, wide_cols), lambda h: (0, h))],
        out_shape=[sds((count, query.shape[0]), BF)] * 2 + [sds((rows, cols), F32)],
        scratch_shapes=[
            pltpu.VMEM((count, HD), BF),
            pltpu.VMEM((count, HD), BF),
            pltpu.VMEM((HD, count), BF),
        ],
        compiler_params=alone,
        cost_estimate=cost(8),
    )(pre, query, mixing, *arrays, cosine, sine, gain)


def attention_back(slope, probs, score_cot, back, query, mixing, cosine, sine, k_pre, k_gain):
    rows, cols = back.shape
    heads = cols // HD
    own_cols = cols + 2 * HD
    send_cols = own_cols + 4 * HD
    count = KV_BLOCKS * rows

    def kernel(slope_ref, probs_ref, score_ref, back_ref, query_ref, mixing_ref, *refs):
        cos_ref, sin_ref, k_pre_ref, k_gain_ref, own_ref, home_ref, *send_refs = refs
        slope = slope_ref[...]
        tall = jnp.concatenate([slope] * heads, axis=0)
        query = (tall * wide(query_ref[...])).astype(BF)
        grad = (tall * mixing_ref[...]).astype(BF)
        key_cot = jnp.dot(score_ref[...], query, preferred_element_type=F32)
        value_cot = jnp.dot(probs_ref[...], grad, preferred_element_type=F32)
        cots = jnp.concatenate([key_cot.astype(BF), value_cot.astype(BF)], axis=1)

        def block(n):
            return cots[n * rows : (n + 1) * rows]

        own_k = turn_back(
            k_pre_ref[...], k_gain_ref[...], cos_ref[...], sin_ref[...], key_cot[count - rows :]
        )
        own = jnp.concatenate(
            [(slope * back_ref[...]).astype(BF), own_k.astype(BF), block(2 * XS)[:, HD:]], axis=1
        )
        own_ref[...] = own
        for n in range(2):
            home_ref[n] = block(n)
        for dx in range(1, XS):
            send_ref = send_refs[dx - 1]
            send_ref[:, :own_cols] = own
            for n in range(2):
                at = own_cols + n * 2 * HD
                send_ref[:, at : at + 2 * HD] = block(2 * (XS - dx) + n)

    send_out = sds((rows, send_cols), BF)
    outs = [sds((rows, own_cols), BF), sds((2, rows, 2 * HD), BF)] + [send_out] * (XS - 1)
    inputs = (slope, probs, score_cot, back, query, mixing, cosine, sine, k_pre, k_gain)
    return pl.pallas_call(
        kernel,
        grid=(1,),
        in_specs=[whole(v) for v in inputs],
        out_specs=[whole(v) for v in outs],
        out_shape=outs,
        compiler_params=alone,
        cost_estimate=cost(4),
    )(*inputs)


def weight_grad(left, blocks, cols, tile):
    def kernel(left_ref, *refs):
        right = jnp.concatenate(
            [r[...].reshape(-1, tile) for r in refs[:-1]], axis=0
        )
        refs[-1][...] = jnp.dot(left_ref[...], right, preferred_element_type=F32).astype(BF)

    specs = [
        pl.BlockSpec(b.shape[:-1] + (tile,), lambda c, n=b.ndim: (0,) * (n - 1) + (c,)) for b in blocks
    ]
    return pl.pallas_call(
        kernel,
        grid=(cols // tile,),
        in_specs=[whole(left)] + specs,
        out_specs=pl.BlockSpec((left.shape[0], tile), lambda c: (0, c)),
        out_shape=sds((left.shape[0], cols), BF),
        compiler_params=params,
        cost_estimate=cost(3),
    )(left, *blocks)


def weight_grad_kv(order, left_x, blocks, left_p, prompt, kcols):
    tile = 2 * kcols
    rows, cols = blocks[0].shape
    at = cols // tile - 1
    count = len(blocks)

    def kernel(order_ref, x_ref, p_ref, *refs):
        k_ref, v_ref, sum_ref = refs[-3:]
        right = jnp.concatenate([r[...] for r in refs[:count]], axis=0)
        total = jnp.dot(x_ref[...], right, preferred_element_type=F32)
        more = [r[...].reshape(-1, tile) for r in refs[count:-3]]
        right = jnp.concatenate([m[:rows] for m in more], axis=0)
        total += jnp.dot(p_ref[...], right, preferred_element_type=F32)
        k_ref[...] = total[:, :kcols].astype(BF)
        v_ref[...] = total[:, kcols:].astype(BF)
        scalars = [scalar_of(m) for m in more]
        added = jnp.zeros((1, 1), F32)
        for device in range(count):
            added += sum(jnp.where(order_ref[n] == device, scalars[n], 0.0) for n in range(count))
        sum_ref[...] = jnp.broadcast_to(added, sum_ref.shape)

    specs = [pl.BlockSpec((rows, tile), lambda c, o: (0, at))] * count
    for array, index in prompt:
        if index is None:
            specs.append(pl.BlockSpec((rows + TAIL, tile), lambda c, o: (0, 0)))
        else:
            specs.append(
                pl.BlockSpec((1, rows + TAIL, tile), lambda c, o, index=index: (index, 0, 0))
            )
    narrow = sds((left_x.shape[0], kcols), BF)
    outs = [narrow, narrow, sds((8, HD), F32)]
    return pl.pallas_call(
        kernel,
        grid_spec=pltpu.PrefetchScalarGridSpec(
            num_scalar_prefetch=1,
            grid=(1,),
            in_specs=[whole(left_x), whole(left_p)] + specs,
            out_specs=[whole(v) for v in outs],
        ),
        out_shape=outs,
        compiler_params=params,
        cost_estimate=cost(3),
    )(order, left_x, left_p, *blocks, *[array for array, _ in prompt])


def tables(positions):
    half = HD // 2
    frequency = jnp.exp(jnp.arange(half, dtype=F32) * (-2.0 * math.log(rope_base) / HD))
    angles = positions[:, None] * frequency[None, :]
    cosine, sine = jnp.cos(angles), jnp.sin(angles)
    return jnp.concatenate([cosine, cosine], axis=1), jnp.concatenate([-sine, sine], axis=1)


def body(
    resp_hidden,
    prompt_hidden,
    readout,
    query_weight,
    key_weight,
    value_weight,
    out_weight,
    query_gain,
    key_gain,
    base_logprob,
    behavior_logprob,
    reference_logprob,
    rewards,
    lengths,
):
    own_x = resp_hidden[0]
    own_read = readout[0]
    rows = own_x.shape[0]
    qcols = query_weight.shape[1]
    kcols = key_weight.shape[1]
    groups = lax.axis_size("resp")
    index = lax.axis_index("resp").astype(jnp.int32)
    offset = jnp.arange(2 * XS, dtype=jnp.int32)
    order = ((index // 2 + offset % XS) % XS) * 2 + (index % 2 + offset // XS) % 2

    packed, own_acc = pack(own_x, prompt_hidden, own_read)
    tokens = exchange(packed)
    own_part = jnp.sum(own_acc, axis=-1)
    prompt_pos = (index * rows + jnp.arange(rows)).astype(F32)
    resp_pos = (rows * groups + jnp.arange(rows)).astype(F32)
    prompt_cos, prompt_sin = tables(prompt_pos)
    resp_cos, resp_sin = tables(resp_pos)

    kv_weight = jnp.concatenate([key_weight, value_weight], axis=1)
    qkv_weight = jnp.concatenate([query_weight, kv_weight], axis=1)
    okv_weight = jnp.concatenate([out_weight, kv_weight], axis=1)
    tiles = qkv_weight.shape[1] // 256

    pairs = list(project(order, tokens, [2] * (tiles - 1) + [1], okv_weight, True))
    got_m = [send(pairs[n], n) for n in range(1, XS)]
    pairs[0], tokens = lax.optimization_barrier((pairs[0], tokens))
    near_q, far_q = project(order, tokens, [0] * tiles, qkv_weight, False)
    got_q = send(far_q, 0, 1)
    far_q, tokens = lax.optimization_barrier((far_q, tokens))
    flipped = flip_tokens(order, tokens)
    got_m, flipped = lax.optimization_barrier((got_m, flipped))
    left_x, left_p, left_r = flipped
    far_m = (wide(pairs[0][1]) + sum(wide(g[1]) for g in got_m)).astype(BF)
    last_m = send(far_m, 0, 1)
    half_q = [(wide(near_q[n]) + wide(got_q[n])).astype(BF) for n in range(1, XS)]
    parts_q = [send(half_q[n - 1], n) for n in range(1, XS)]
    kv_pre = wide(pairs[0][0, :, qcols:]) + sum(wide(g[0, :, qcols:]) for g in got_m)
    kv_pre = kv_pre + wide(last_m[:, qcols:])
    kp_pre = kv_pre[:, :kcols]
    prompt_keys = norm_rope(kp_pre, key_gain, prompt_pos)
    kv_block = jnp.concatenate([prompt_keys.astype(BF), kv_pre[:, kcols:].astype(BF)], axis=1)
    kv_block = with_scalar(kv_block, rewards[0])
    other_kv = send(kv_block, 0, 1)
    parts_q, kv_block, other_kv = lax.optimization_barrier((parts_q, kv_block, other_kv))
    pair_kv = jnp.stack([kv_block, other_kv])
    got_kv = [send(pair_kv, n) for n in range(1, XS)]
    kvr_pre = wide(near_q[0][:, qcols:]) + wide(got_q[0][:, qcols:])
    kvr_pre = kvr_pre + sum(wide(part[:, qcols:]) for part in parts_q)
    kr_pre = kvr_pre[:, :kcols]
    resp_keys = norm_rope(kr_pre, key_gain, resp_pos)
    own_kv = jnp.concatenate([resp_keys.astype(BF), kvr_pre[:, kcols:].astype(BF)], axis=1)
    prompt_kv = [kv_block, other_kv] + got_kv

    q_gain, k_gain = query_gain[None, :], key_gain[None, :]
    q_pre, query, mixed, mixing, attn_acc, reward_sum = attention(
        (near_q, got_q),
        parts_q,
        [pairs[0]] + got_m,
        last_m,
        prompt_kv,
        own_kv,
        resp_cos,
        resp_sin,
        q_gain,
    )
    probs, score_cot, back = attention_slopes(
        q_pre, query, mixing, prompt_kv, own_kv, resp_cos, resp_sin, q_gain
    )
    attn_logit = xor_sum(jnp.sum(attn_acc, axis=-1)[None, :], "head")[0]
    logprob = base_logprob[0] + own_part + attn_logit
    advantage = rewards[0] - reward_sum[0, 0] / groups
    live = (jnp.arange(rows) < lengths[0]).astype(F32)
    loss_own, lp_slope = objective(
        logprob, behavior_logprob[0], reference_logprob[0], advantage, live
    )
    mixing_grad = (lp_slope[:, None] * wide(mixed)).astype(BF)
    near_dm = [mixing_grad] + [send(mixing_grad, XS - n) for n in range(1, XS)]
    own_cots, home, *send_cots = attention_back(
        lp_slope[:, None],
        probs,
        score_cot,
        back,
        query,
        mixing,
        resp_cos,
        resp_sin,
        kr_pre,
        k_gain,
    )
    first_dm = send(mixing_grad, 0, 1)
    own_cots, home, send_cots, near_dm, first_dm = lax.optimization_barrier(
        (own_cots, home, send_cots, near_dm, first_dm)
    )
    got_d = [send(send_cots[n], n + 1) for n in range(XS - 1)]
    other_cots = send(own_cots, 0, 1)
    far_dm = send(jnp.stack(near_dm[1:]), 0, 1)
    got_d, other_cots, far_dm = lax.optimization_barrier((got_d, other_cots, far_dm))
    at = qcols + 2 * kcols
    far_kv = (wide(home[1]) + sum(wide(g[:, at + 2 * kcols :]) for g in got_d)).astype(BF)
    last_kv = send(far_kv, 0, 1)
    far_d = [send(other_cots, n) for n in range(1, XS)]
    dkv = wide(home[0]) + sum(wide(g[:, at : at + 2 * kcols]) for g in got_d) + wide(last_kv)
    dkp = turn_back(kp_pre, k_gain, prompt_cos, prompt_sin, dkv[:, :kcols])
    block_dp = jnp.concatenate([dkp.astype(BF), dkv[:, kcols:].astype(BF)], axis=1)
    block_dp = with_scalar(block_dp, loss_own)
    other_dp = send(block_dp, 0, 1)
    out_grad = weight_grad(left_r, near_dm + [first_dm, far_dm], qcols, 512)
    far_d, other_dp, out_grad = lax.optimization_barrier((far_d, other_dp, out_grad))
    pair_dp = jnp.stack([block_dp, other_dp])
    got_dp = [send(pair_dp, n) for n in range(1, XS)]
    by_offset = [2, 1, 0]
    cots = [own_cots] + [got_d[n] for n in by_offset]
    cots += [other_cots] + [far_d[n] for n in by_offset]
    query_grad = weight_grad(left_x, cots, qcols, 512)
    got_dp, query_grad = lax.optimization_barrier((got_dp, query_grad))
    prompt = [(block_dp, None)] + [(got_dp[n], 0) for n in by_offset]
    prompt += [(other_dp, None)] + [(got_dp[n], 1) for n in by_offset]
    key_grad, value_grad, loss = weight_grad_kv(order, left_x, cots, left_p, prompt, kcols)
    group_loss = loss[0, :1]
    return (
        logprob[None, :],
        group_loss,
        query_grad,
        key_grad,
        value_grad,
        out_grad,
    )


def solution(mesh):
    placed = (
        P(("grp", "resp"), None, None),
        P(("grp", "resp"), None),
        P(("grp", "resp"), None, None),
        P("resp", "head"),
        P("resp", "head"),
        P("resp", "head"),
        P("resp", "head"),
        P(),
        P(),
        P(("grp", "resp"), None),
        P(("grp", "resp"), None),
        P(("grp", "resp"), None),
        P(("grp", "resp")),
        P(("grp", "resp")),
    )
    return jax.shard_map(
        body,
        mesh=mesh,
        in_specs=placed,
        out_specs=(
            P(("grp", "resp"), None),
            P("grp"),
            P(("grp", "resp"), "head"),
            P(("grp", "resp"), "head"),
            P(("grp", "resp"), "head"),
            P(("grp", "resp"), "head"),
        ),
        check_vma=False,
    )
```

time: 339 us -> 261 us (0.77)
  blocking collectives: 53.8 us -> 0 us
  Pallas kernels: 0 us -> 50.1 us
  matrix products: 34 us -> 0 us
  waiting for transfers between devices: 130 us -> 108 us
  local copies, waits for them, and re-layouts: 26.5 us -> 5.81 us
  other arithmetic: 27.1 us -> 16 us
  starting transfers between devices: 56.5 us -> 67.3 us
  between operations: 8.28 us -> 11.7 us
    all_to_all x1 -> x0, blocking collectives: 53.8 us -> none  [exchange(): lax.all_to_all(blocks, 'resp', split_axis=0, concat_axis=0, tiled=True)]
    pallas_call x0 -> x10, Pallas kernels: none -> 50.1 us  [the longest x2 13 us: project(): pl.pallas_call(kernel, grid_spec=pltpu.PrefetchScalarGridSpec(num_scalar_...]
    dot_general x16 -> x0, matrix products: 34 us -> none  [the longest x4 12.7 us: weight_grad(): jnp.einsum('ntd,ntc->dc', left, right, preferred_element_type=jnp.float32)]
    all_to_all x4 -> x1, waiting for transfers between devices: 78.2 us -> 44.8 us  [exchange(): lax.all_to_all(blocks, 'resp', split_axis=0, concat_axis=0, tiled=True)]
    ppermute x9 -> x33, starting transfers between devices: 31.9 us -> 59.6 us  [the longest x29 49.8 us: send(): return lax.ppermute(value, 'resp', pairs)]
    all_to_all x4 -> x1, starting transfers between devices: 24.6 us -> 7.74 us  [exchange(): lax.all_to_all(blocks, 'resp', split_axis=0, concat_axis=0, tiled=True)]
    ppermute x9 -> x33, waiting for transfers between devices: 51.7 us -> 62.9 us  [the longest x29 57.9 us: send(): return lax.ppermute(value, 'resp', pairs)]
    unnamed x84 -> x82, local copies, waits for them, and re-layouts: 9.79 us -> 2.76 us
  transfers between devices with their start and end apart: 13 -> 34, of which waited for: 8 -> 15; matrix products, arithmetic and copies ran while one was open for 4% -> 6% of each run, Pallas kernels for 0% -> 12%
where the time goes in v2:
time: 261 us; the launch traced here: 259 us
  waiting for transfers between devices  108 us (41%)
  starting transfers between devices  67.3 us (26%)
  Pallas kernels  50.1 us (19%)
  other arithmetic  16 us (6%)
  between operations  11.7 us (4%)
  local copies, waits for them, and re-layouts  5.81 us (2%)
    ppermute x29, waiting for transfers between devices, send(): return lax.ppermute(value, 'resp', pairs)  57.9 us
    ppermute x29, starting transfers between devices, send(): return lax.ppermute(value, 'resp', pairs)  49.8 us
    all_to_all x1, waiting for transfers between devices, exchange(): lax.all_to_all(blocks, 'resp', split_axis=0, concat_axis=0, tiled=True)  44.8 us
    pallas_call x2, Pallas kernels, project(): pl.pallas_call(kernel, grid_spec=pltpu.PrefetchScalarGridSpec(num_scalar_...  13 us
    ppermute x4, starting transfers between devices, flip(): return lax.ppermute(term, axis, [(i, i ^ step) for i in range(2 * XS)])  9.76 us
    all_to_all x1, starting transfers between devices, exchange(): lax.all_to_all(blocks, 'resp', split_axis=0, concat_axis=0, tiled=True)  7.74 us
    pallas_call x2, Pallas kernels, weight_grad(): pl.pallas_call(kernel, grid=(cols // tile,), in_specs=[whole(left)] + spe...  6.77 us
    pallas_call x1, Pallas kernels, attention_slopes(): pl.pallas_call(kernel, grid=(cols // wide_cols,), in_specs=[tall] * 3 + s...  6.49 us
  transfers between devices with their start and end apart: 34, of which 15 were waited for; matrix products, arithmetic and copies ran while one was open for 6% of the time, Pallas kernels for 12%

profile of v2, /device:TPU:2, one launch (start us, length us, event | category | flops | bytes accessed | tf_op | source)
XLA Modules:
  0.0 258.6 jit_solution(11488420196094574838)
XLA Ops:
  0.6 4.8 %shard_map.181 = (bf16[8,384,640]{2,1,0:T(8,128)(2,1)}, f32[128,128]{1,0:T(8,128)}) custom-call(bf16[128,5120]{1,0:T(8,128)(2,1)} %bitcast.103, bf16[128,5120]{1,0:T(8,128)(2,1)} %p_ref.1, bf16[128,5120]{1,0:T(8,128)(2,1)} %bitcast.104), custom_call_target="tpu_custom_call" | custom-call | flops 400000000 | bytes 262144 | tf_op jit(solution)/shard_map/pallas_call | solution.py:135
  5.4 7.7 %all-to-all-start = ((bf16[8,384,640]{2,1,0:T(8,128)(2,1)}), bf16[8,384,640]{2,1,0:T(8,128)(2,1)}, u32[]{:S(2)}, u32[]{:S(2)}) async-start(bf16[8,384,640]{2,1,0:T(8,128)(2,1)} %get-tuple-element.97), calls=%async_computation | async-start | bytes 7864320 | tf_op jit(solution)/shard_map/all_to_all | solution.py:110
  21.5 44.8 %all-to-all-done.refs_0_.refs_1_.refs_2_.refs_3_.refs_4_.refs_5_.refs_6_.refs_7_.refs_8_.refs_9_.refs_10_.refs_11_.refs_12_.refs_13_.refs_14_.refs_15_.tokens_ref = bf16[8,384,640]{2,1,0:T(8,128)(2,1)} async-done(((bf16[8,384,640]{2,1,0:T(8,128)(2,1)}), bf16[8,384,640]{2,1,0:T(8,128)(2,1)}, u32[]{:S(2)}, u32[]{:S(2)}) %all-to-all-start) | async-done | bytes 3932192 | tf_op jit(solution)/shard_map/all_to_all | solution.py:110
  66.3 6.7 %shard_map.182 = (bf16[2,128,1280]{2,1,0:T(8,128)(2,1)}, bf16[2,128,1280]{2,1,0:T(8,128)(2,1)}, bf16[2,128,1280]{2,1,0:T(8,128)(2,1)}, bf16[2,128,1280]{2,1,0:T(8,128)(2,1)}) custom-call(s32[8]{0:T(128)} %fusion.43.order_ref, ...), custom_call_target="tpu_custom_call" | custom-call | flops 400000000 | bytes 262144 | tf_op jit(solution)/shard_map/pallas_call | solution.py:177
  74.0 4.0 %collective-permute-start.5 = (bf16[2,128,1280]{2,1,0:T(8,128)(2,1)}, bf16[2,128,1280]{2,1,0:T(8,128)(2,1)S(1)}, u32[]{:S(2)}, u32[]{:S(2)}) collective-permute-start(bf16[2,128,1280]{2,1,0:T(8,128)(2,1)} %get-tuple-element.104), channel_id=1, source_target_pairs={{0,32},{8,40},{16,48},{24,56},{32,0},{40,8},{48,16},{56,24},{1,33}... | collective-permute-start | bytes 1966088 | tf_op jit(solution)/shard_map/ppermute | solution.py:85
  80.6 6.3 %shard_map.183 = (bf16[4,128,1280]{2,1,0:T(8,128)(2,1)}, bf16[4,128,1280]{2,1,0:T(8,128)(2,1)}) custom-call(s32[8]{0:T(128)} %fusion.43.order_ref, bf16[8,384,640]{2,1,0:T(8,128)(2,1)} %all-to-all-done.refs_0_.refs_1_.refs_2_.refs_3_.refs_4_.refs_5_.refs_6_.refs_7_.refs_8_.refs_9_.refs_10_.refs_11_.refs_12_.refs_13_.refs_14_.refs_15_.tokens_ref, ...), custom_call_target="tpu_custom_call" | custom-call | flops 400000000 | bytes 262144 | tf_op jit(solution)/shard_map/pallas_call | solution.py:177
  89.6 6.3 %shard_map.184 = (bf16[640,1024]{1,0:T(8,128)(2,1)S(1)}, bf16[640,1024]{1,0:T(8,128)(2,1)S(1)}, bf16[640,1024]{1,0:T(8,128)(2,1)S(1)}) custom-call(s32[8]{0:T(128)S(1)} %copy-done.11, bf16[8,384,640]{2,1,0:T(8,128)(2,1)} %all-to-all-done.refs_0_.refs_1_.refs_2_.refs_3_.refs_4_.refs_5_.refs_6_.refs_7_.refs_8_.refs_9_.refs_10_.refs_11_.refs_12_.refs_13_.refs_14_.refs_15_.tokens_ref), custom_call_target="tpu_custom_call" | custom-call | flops 800000000 | bytes 262144 | tf_op jit(solution)/shard_map/pallas_call | solution.py:202
  96.0 10.2 %collective-permute-done.6.refs_8_ = bf16[2,128,1280]{2,1,0:T(8,128)(2,1)S(1)} collective-permute-done((bf16[2,128,1280]{2,1,0:T(8,128)(2,1)}, bf16[2,128,1280]{2,1,0:T(8,128)(2,1)S(1)}, u32[]{:S(2)}, u32[]{:S(2)}) %collective-permute-start.6) | collective-permute-done | bytes 655392 | tf_op jit(solution)/shard_map/ppermute | solution.py:85
  108.1 16.1 %collective-permute-done.7.refs_9_ = bf16[128,1280]{1,0:T(8,128)(2,1)S(1)} collective-permute-done((bf16[128,1280]{1,0:T(8,128)(2,1)S(1)}, bf16[128,1280]{1,0:T(8,128)(2,1)S(1)}, u32[]{:S(2)}, u32[]{:S(2)}) %collective-permute-start.7) | collective-permute-done | bytes 327712 | tf_op jit(solution)/shard_map/ppermute | solution.py:85
  132.1 6.7 %collective-permute-done.1.refs_2_ = bf16[128,1280]{1,0:T(8,128)(2,1)S(1)} collective-permute-done((bf16[128,1280]{1,0:T(8,128)(2,1)S(1)}, bf16[128,1280]{1,0:T(8,128)(2,1)S(1)}, u32[]{:S(2)}, u32[]{:S(2)}) %collective-permute-start.1) | collective-permute-done | bytes 327712 | tf_op jit(solution)/shard_map/ppermute | solution.py:85
  141.1 3.3 %collective-permute-done.3.refs_4_ = bf16[128,1280]{1,0:T(8,128)(2,1)S(1)} collective-permute-done((bf16[128,1280]{1,0:T(8,128)(2,1)S(1)}, bf16[128,1280]{1,0:T(8,128)(2,1)S(1)}, u32[]{:S(2)}, u32[]{:S(2)}) %collective-permute-start.3) | collective-permute-done | bytes 327712 | tf_op jit(solution)/shard_map/ppermute | solution.py:85
  154.2 5.0 %shard_map.185 = (f32[1024,128]{1,0:T(8,128)}, bf16[1024,128]{1,0:T(8,128)(2,1)}, bf16[128,1024]{1,0:T(8,128)(2,1)}, f32[1024,128]{1,0:T(8,128)}, f32[128,128]{1,0:T(8,128)}, /*index=5*/f32[8,128]{1,0:T(8,128)}) custom-call(bf16[4,128,1280]{2,1,0:T(8,128)(2,1)} %get-tuple-element.100.refs_0_, bf16[4,128,1280]{2,1,0:T(8,128)(2,1)} %copy-done.13, ...), custom_call_target="tpu_custom_call" | custom-call | flops 800000000 | bytes 262144 | tf_op jit(solution)/shard_map/pallas_call | solution.py:314
  162.2 3.3 %collective-permute-start.13 = (f32[1,128]{1,0:T(1,128)S(1)}, f32[1,128]{1,0:T(1,128)S(1)}, u32[]{:S(2)}, u32[]{:S(2)}) collective-permute-start(f32[1,128]{1,0:T(1,128)S(1)} %bitcast.114), channel_id=1, source_target_pairs={{0,2},{1,3},{2,0},{3,1},{4,6},{5,7},{6,4},{7,5},{8,10},{9,11},{10,... | collective-permute-start | bytes 1544 | tf_op jit(solution)/shard_map/ppermute | solution.py:90
  167.0 3.8 %collective-permute-done.14 = f32[1,128]{1,0:T(1,128)S(1)} collective-permute-done((f32[1,128]{1,0:T(1,128)S(1)}, f32[1,128]{1,0:T(1,128)S(1)}, u32[]{:S(2)}, u32[]{:S(2)}) %collective-permute-start.14) | collective-permute-done | bytes 544 | tf_op jit(solution)/shard_map/ppermute | solution.py:90
  170.8 4.5 %collective-permute-start.15 = (f32[1,128]{1,0:T(1,128)S(1)}, f32[1,128]{1,0:T(1,128)S(1)}, u32[]{:S(2)}, u32[]{:S(2)}) collective-permute-start(f32[1,128]{1,0:T(1,128)S(1)} %add_add_fusion.1), channel_id=1, source_target_pairs={{0,4},{1,5},{2,6},{3,7},{4,0},{5,1},{6,2},{7,3},{8,12},{9,13},{10,... | collective-permute-start | bytes 1544 | tf_op jit(solution)/shard_map/ppermute | solution.py:90
  175.3 6.5 %shard_map.186 = (bf16[1152,1024]{1,0:T(8,128)(2,1)}, bf16[1152,1024]{1,0:T(8,128)(2,1)}, f32[128,1024]{1,0:T(8,128)}) custom-call(f32[1024,128]{1,0:T(8,128)} %get-tuple-element.122.pre_ref, bf16[1024,128]{1,0:T(8,128)(2,1)} %get-tuple-element.123.query_ref, f32[1024,128]{1,0:T(8,128)} %get-tuple-element.124.mixing_ref, bf16[144,256]{1,0:T(8,128)(2,1)} %copy-done.21, ...), custom_call_target="tpu_custom_call" | custom-call | flops 800000000 | bytes 262144 | tf_op jit(solution)/shard_map/pallas_call | solution.py:367
  189.1 3.0 %collective-permute-start.19 = (bf16[128,1024]{1,0:T(8,128)(2,1)S(1)}, bf16[128,1024]{1,0:T(8,128)(2,1)S(1)}, u32[]{:S(2)}, u32[]{:S(2)}) collective-permute-start(bf16[128,1024]{1,0:T(8,128)(2,1)S(1)} %multiply_convert_fusion.refs_0_), channel_id=1, source_target_pairs={{0,8},{8,0},{16,24},{24,16},{32,40},{40,32},{48,56},{56,48},{1,9},... | collective-permute-start | bytes 786440 | tf_op jit(solution)/shard_map/ppermute | solution.py:85
  193.0 5.6 %shard_map.187 = (bf16[128,1280]{1,0:T(8,128)(2,1)}, bf16[2,128,256]{2,1,0:T(8,128)(2,1)}, bf16[128,1792]{1,0:T(8,128)(2,1)}, bf16[128,1792]{1,0:T(8,128)(2,1)}, bf16[128,1792]{1,0:T(8,128)(2,1)}) custom-call(f32[128,1]{1,0:T(8,128)} %subtract_select_fusion.slope_ref, bf16[1152,1024]{1,0:T(8,128)(2,1)} %get-tuple-element.125.probs_ref, ...), custom_call_target="tpu_custom_call" | custom-call | flops 400000000 | bytes 262144 | tf_op jit(solution)/shard_map/pallas_call | solution.py:422
  202.4 3.6 %collective-permute-start.21 = (bf16[128,1792]{1,0:T(8,128)(2,1)}, bf16[128,1792]{1,0:T(8,128)(2,1)S(1)}, u32[]{:S(2)}, u32[]{:S(2)}) collective-permute-start(bf16[128,1792]{1,0:T(8,128)(2,1)} %get-tuple-element.136), channel_id=1, source_target_pairs={{0,32},{8,40},{16,48},{24,56},{32,0},{40,8},{48,16},{56,24},{1,33}... | collective-permute-start | bytes 1376264 | tf_op jit(solution)/shard_map/ppermute | solution.py:85
  211.7 12.4 %collective-permute-done.23.refs_4_ = bf16[128,1280]{1,0:T(8,128)(2,1)S(1)} collective-permute-done((bf16[128,1280]{1,0:T(8,128)(2,1)}, bf16[128,1280]{1,0:T(8,128)(2,1)S(1)}, u32[]{:S(2)}, u32[]{:S(2)}) %collective-permute-start.23) | collective-permute-done | bytes 327712 | tf_op jit(solution)/shard_map/ppermute | solution.py:85
  229.7 4.2 %collective-permute-start.26 = (bf16[128,1280]{1,0:T(8,128)(2,1)S(1)}, bf16[128,1280]{1,0:T(8,128)(2,1)S(1)}, u32[]{:S(2)}, u32[]{:S(2)}) collective-permute-start(bf16[128,1280]{1,0:T(8,128)(2,1)S(1)} %collective-permute-done.23.refs_4_), channel_id=1, source_target_pairs={{0,32},{8,40},{16,48},{24,56},{32,0},{40,8},{48,16},{56,24},{1,33}... | collective-permute-start | bytes 983048 | tf_op jit(solution)/shard_map/ppermute | solution.py:85
  239.8 3.6 %shard_map.188 = bf16[640,1024]{1,0:T(8,128)(2,1)} custom-call(bf16[640,1024]{1,0:T(8,128)(2,1)S(1)} %copy-done.1, bf16[128,1024]{1,0:T(8,128)(2,1)S(1)} %multiply_convert_fusion.refs_0_, bf16[128,1024]{1,0:T(8,128)(2,1)S(1)} %collective-permute-done.16.refs_1_, bf16[128,1024]{1,0:T(8,128)(2,1)S(1)} %copy-done.6, bf16[128,1024]{1,0:T(8,128)(2,1)S(1)} %copy-done.8, ...), custom_call_target="tpu_custom_call" | custom-call | flops 300000000 | bytes 262144 | tf_op jit(solution)/shard_map/pallas_call | solution.py:443
  246.7 3.2 %collective-permute-start.31 = (bf16[2,144,256]{2,1,0:T(8,128)(2,1)S(1)}, bf16[2,144,256]{2,1,0:T(8,128)(2,1)S(1)}, u32[]{:S(2)}, u32[]{:S(2)}) collective-permute-start(bf16[2,144,256]{2,1,0:T(8,128)(2,1)S(1)} %pad_maximum_fusion.6), channel_id=1, source_target_pairs={{0,32},{8,40},{16,48},{24,56},{32,0},{40,8},{48,16},{56,24},{1,33}... | collective-permute-start | bytes 442376 | tf_op jit(solution)/shard_map/ppermute | solution.py:85
  252.2 3.2 %shard_map.189 = bf16[640,1024]{1,0:T(8,128)(2,1)} custom-call(bf16[640,1024]{1,0:T(8,128)(2,1)S(1)} %get-tuple-element.119.left_ref.x_ref, bf16[128,1280]{1,0:T(8,128)(2,1)S(1)} %copy-done.2, bf16[128,1792]{1,0:T(8,128)(2,1)S(1)} %collective-permute-done.22.refs_1_, bf16[128,1792]{1,0:T(8,128)(2,1)S(1)} %collective-permute-done.21.refs_2_, ...), custom_call_target="tpu_custom_call" | custom-call | flops 300000000 | bytes 262144 | tf_op jit(solution)/shard_map/pallas_call | solution.py:443
  (191 shorter events, 68.1 us)
Async XLA Ops:
  5.4 60.8 %all-to-all-start = ((bf16[8,384,640]{2,1,0:T(8,128)(2,1)}), bf16[8,384,640]{2,1,0:T(8,128)(2,1)}, u32[]{:S(2)}, u32[]{:S(2)}) async-start(bf16[8,384,640]{2,1,0:T(8,128)(2,1)} %get-tuple-element.97), calls=%async_computation | async-start | bytes 7864320 | tf_op jit(solution)/shard_map/all_to_all | solution.py:110
  73.0 23.0 %collective-permute-start.4 = (bf16[2,128,1280]{2,1,0:T(8,128)(2,1)}, bf16[2,128,1280]{2,1,0:T(8,128)(2,1)S(1)}, u32[]{:S(2)}, u32[]{:S(2)}) collective-permute-start(bf16[2,128,1280]{2,1,0:T(8,128)(2,1)} %get-tuple-element.103), channel_id=1, source_target_pairs={{0,16},{8,24},{16,32},{24,40},{32,48},{40,56},{48,0},{56,8},{1,17}... | collective-permute-start | bytes 1966088 | tf_op jit(solution)/shard_map/ppermute | solution.py:85
  74.0 21.9 %collective-permute-start.5 = (bf16[2,128,1280]{2,1,0:T(8,128)(2,1)}, bf16[2,128,1280]{2,1,0:T(8,128)(2,1)S(1)}, u32[]{:S(2)}, u32[]{:S(2)}) collective-permute-start(bf16[2,128,1280]{2,1,0:T(8,128)(2,1)} %get-tuple-element.104), channel_id=1, source_target_pairs={{0,32},{8,40},{16,48},{24,56},{32,0},{40,8},{48,16},{56,24},{1,33}... | collective-permute-start | bytes 1966088 | tf_op jit(solution)/shard_map/ppermute | solution.py:85
  78.0 28.1 %collective-permute-start.6 = (bf16[2,128,1280]{2,1,0:T(8,128)(2,1)}, bf16[2,128,1280]{2,1,0:T(8,128)(2,1)S(1)}, u32[]{:S(2)}, u32[]{:S(2)}) collective-permute-start(bf16[2,128,1280]{2,1,0:T(8,128)(2,1)} %get-tuple-element.105), channel_id=1, source_target_pairs={{0,48},{8,56},{16,0},{24,8},{32,16},{40,24},{48,32},{56,40},{1,49}... | collective-permute-start | bytes 1966088 | tf_op jit(solution)/shard_map/ppermute | solution.py:85
  86.9 41.8 %collective-permute-start = (bf16[4,128,1280]{2,1,0:T(8,128)(2,1)}, bf16[4,128,1280]{2,1,0:T(8,128)(2,1)S(1)}, u32[]{:S(2)}, u32[]{:S(2)}) collective-permute-start(bf16[4,128,1280]{2,1,0:T(8,128)(2,1)} %get-tuple-element.101), channel_id=1, source_target_pairs={{0,8},{8,0},{16,24},{24,16},{32,40},{40,32},{48,56},{56,48},{1,9},... | collective-permute-start | bytes 3932168 | tf_op jit(solution)/shard_map/ppermute | solution.py:85
  106.3 17.8 %collective-permute-start.7 = (bf16[128,1280]{1,0:T(8,128)(2,1)S(1)}, bf16[128,1280]{1,0:T(8,128)(2,1)S(1)}, u32[]{:S(2)}, u32[]{:S(2)}) collective-permute-start(bf16[128,1280]{1,0:T(8,128)(2,1)S(1)} %fusion.3), channel_id=1, source_target_pairs={{0,8},{8,0},{16,24},{24,16},{32,40},{40,32},{48,56},{56,48},{1,9},... | collective-permute-start | bytes 983048 | tf_op jit(solution)/shard_map/ppermute | solution.py:85
  129.0 9.8 %collective-permute-start.1 = (bf16[128,1280]{1,0:T(8,128)(2,1)S(1)}, bf16[128,1280]{1,0:T(8,128)(2,1)S(1)}, u32[]{:S(2)}, u32[]{:S(2)}) collective-permute-start(bf16[128,1280]{1,0:T(8,128)(2,1)S(1)} %get-tuple-element.168), channel_id=1, source_target_pairs={{0,16},{8,24},{16,32},{24,40},{32,48},{40,56},{48,0},{56,8},{1,17}... | collective-permute-start | bytes 983048 | tf_op jit(solution)/shard_map/ppermute | solution.py:85
  129.9 11.1 %collective-permute-start.2 = (bf16[128,1280]{1,0:T(8,128)(2,1)S(1)}, bf16[128,1280]{1,0:T(8,128)(2,1)S(1)}, u32[]{:S(2)}, u32[]{:S(2)}) collective-permute-start(bf16[128,1280]{1,0:T(8,128)(2,1)S(1)} %get-tuple-element.167), channel_id=1, source_target_pairs={{0,32},{8,40},{16,48},{24,56},{32,0},{40,8},{48,16},{56,24},{1,33}... | collective-permute-start | bytes 983048 | tf_op jit(solution)/shard_map/ppermute | solution.py:85
  131.4 13.0 %collective-permute-start.3 = (bf16[128,1280]{1,0:T(8,128)(2,1)S(1)}, bf16[128,1280]{1,0:T(8,128)(2,1)S(1)}, u32[]{:S(2)}, u32[]{:S(2)}) collective-permute-start(bf16[128,1280]{1,0:T(8,128)(2,1)S(1)} %get-tuple-element.166), channel_id=1, source_target_pairs={{0,48},{8,56},{16,0},{24,8},{32,16},{40,24},{48,32},{56,40},{1,49}... | collective-permute-start | bytes 983048 | tf_op jit(solution)/shard_map/ppermute | solution.py:85
  170.8 12.8 %collective-permute-start.15 = (f32[1,128]{1,0:T(1,128)S(1)}, f32[1,128]{1,0:T(1,128)S(1)}, u32[]{:S(2)}, u32[]{:S(2)}) collective-permute-start(f32[1,128]{1,0:T(1,128)S(1)} %add_add_fusion.1), channel_id=1, source_target_pairs={{0,4},{1,5},{2,6},{3,7},{4,0},{5,1},{6,2},{7,3},{8,12},{9,13},{10,... | collective-permute-start | bytes 1544 | tf_op jit(solution)/shard_map/ppermute | solution.py:90
  184.4 14.1 %collective-permute-start.16 = (bf16[128,1024]{1,0:T(8,128)(2,1)S(1)}, bf16[128,1024]{1,0:T(8,128)(2,1)S(1)}, u32[]{:S(2)}, u32[]{:S(2)}) collective-permute-start(bf16[128,1024]{1,0:T(8,128)(2,1)S(1)} %multiply_convert_fusion.refs_0_), channel_id=1, source_target_pairs={{0,48},{8,56},{16,0},{24,8},{32,16},{40,24},{48,32},{56,40},{1,49}... | collective-permute-start | bytes 786440 | tf_op jit(solution)/shard_map/ppermute | solution.py:85
  186.8 11.8 %collective-permute-start.17 = (bf16[128,1024]{1,0:T(8,128)(2,1)S(1)}, bf16[128,1024]{1,0:T(8,128)(2,1)S(1)}, u32[]{:S(2)}, u32[]{:S(2)}) collective-permute-start(bf16[128,1024]{1,0:T(8,128)(2,1)S(1)} %multiply_convert_fusion.refs_0_), channel_id=1, source_target_pairs={{0,32},{8,40},{16,48},{24,56},{32,0},{40,8},{48,16},{56,24},{1,33}... | collective-permute-start | bytes 786440 | tf_op jit(solution)/shard_map/ppermute | solution.py:85
  187.2 11.4 %collective-permute-start.18 = (bf16[128,1024]{1,0:T(8,128)(2,1)S(1)}, bf16[128,1024]{1,0:T(8,128)(2,1)S(1)}, u32[]{:S(2)}, u32[]{:S(2)}) collective-permute-start(bf16[128,1024]{1,0:T(8,128)(2,1)S(1)} %multiply_convert_fusion.refs_0_), channel_id=1, source_target_pairs={{0,16},{8,24},{16,32},{24,40},{32,48},{40,56},{48,0},{56,8},{1,17}... | collective-permute-start | bytes 786440 | tf_op jit(solution)/shard_map/ppermute | solution.py:85
  189.1 9.4 %collective-permute-start.19 = (bf16[128,1024]{1,0:T(8,128)(2,1)S(1)}, bf16[128,1024]{1,0:T(8,128)(2,1)S(1)}, u32[]{:S(2)}, u32[]{:S(2)}) collective-permute-start(bf16[128,1024]{1,0:T(8,128)(2,1)S(1)} %multiply_convert_fusion.refs_0_), channel_id=1, source_target_pairs={{0,8},{8,0},{16,24},{24,16},{32,40},{40,32},{48,56},{56,48},{1,9},... | collective-permute-start | bytes 786440 | tf_op jit(solution)/shard_map/ppermute | solution.py:85
  199.7 25.1 %collective-permute-start.24 = (bf16[3,128,1024]{2,1,0:T(8,128)(2,1)}, bf16[3,128,1024]{2,1,0:T(8,128)(2,1)}, u32[]{:S(2)}, u32[]{:S(2)}) collective-permute-start(bf16[3,128,1024]{2,1,0:T(8,128)(2,1)} %pad_maximum_fusion.4), channel_id=1, source_target_pairs={{0,8},{8,0},{16,24},{24,16},{32,40},{40,32},{48,56},{56,48},{1,9},... | collective-permute-start | bytes 2359304 | tf_op jit(solution)/shard_map/ppermute | solution.py:85
  201.0 23.1 %collective-permute-start.20 = (bf16[128,1792]{1,0:T(8,128)(2,1)}, bf16[128,1792]{1,0:T(8,128)(2,1)S(1)}, u32[]{:S(2)}, u32[]{:S(2)}) collective-permute-start(bf16[128,1792]{1,0:T(8,128)(2,1)} %get-tuple-element.135), channel_id=1, source_target_pairs={{0,16},{8,24},{16,32},{24,40},{32,48},{40,56},{48,0},{56,8},{1,17}... | collective-permute-start | bytes 1376264 | tf_op jit(solution)/shard_map/ppermute | solution.py:85
  202.4 21.7 %collective-permute-start.21 = (bf16[128,1792]{1,0:T(8,128)(2,1)}, bf16[128,1792]{1,0:T(8,128)(2,1)S(1)}, u32[]{:S(2)}, u32[]{:S(2)}) collective-permute-start(bf16[128,1792]{1,0:T(8,128)(2,1)} %get-tuple-element.136), channel_id=1, source_target_pairs={{0,32},{8,40},{16,48},{24,56},{32,0},{40,8},{48,16},{56,24},{1,33}... | collective-permute-start | bytes 1376264 | tf_op jit(solution)/shard_map/ppermute | solution.py:85
  205.9 18.9 %collective-permute-start.22 = (bf16[128,1792]{1,0:T(8,128)(2,1)}, bf16[128,1792]{1,0:T(8,128)(2,1)S(1)}, u32[]{:S(2)}, u32[]{:S(2)}) collective-permute-start(bf16[128,1792]{1,0:T(8,128)(2,1)} %get-tuple-element.137), channel_id=1, source_target_pairs={{0,48},{8,56},{16,0},{24,8},{32,16},{40,24},{48,32},{56,40},{1,49}... | collective-permute-start | bytes 1376264 | tf_op jit(solution)/shard_map/ppermute | solution.py:85
  206.3 17.8 %collective-permute-start.23 = (bf16[128,1280]{1,0:T(8,128)(2,1)}, bf16[128,1280]{1,0:T(8,128)(2,1)S(1)}, u32[]{:S(2)}, u32[]{:S(2)}) collective-permute-start(bf16[128,1280]{1,0:T(8,128)(2,1)} %get-tuple-element.134.refs_0_), channel_id=1, source_target_pairs={{0,8},{8,0},{16,24},{24,16},{32,40},{40,32},{48,56},{56,48},{1,9},... | collective-permute-start | bytes 983048 | tf_op jit(solution)/shard_map/ppermute | solution.py:85
  227.1 16.6 %collective-permute-start.25 = (bf16[128,1280]{1,0:T(8,128)(2,1)S(1)}, bf16[128,1280]{1,0:T(8,128)(2,1)S(1)}, u32[]{:S(2)}, u32[]{:S(2)}) collective-permute-start(bf16[128,1280]{1,0:T(8,128)(2,1)S(1)} %collective-permute-done.23.refs_4_), channel_id=1, source_target_pairs={{0,16},{8,24},{16,32},{24,40},{32,48},{40,56},{48,0},{56,8},{1,17}... | collective-permute-start | bytes 983048 | tf_op jit(solution)/shard_map/ppermute | solution.py:85
  229.7 14.0 %collective-permute-start.26 = (bf16[128,1280]{1,0:T(8,128)(2,1)S(1)}, bf16[128,1280]{1,0:T(8,128)(2,1)S(1)}, u32[]{:S(2)}, u32[]{:S(2)}) collective-permute-start(bf16[128,1280]{1,0:T(8,128)(2,1)S(1)} %collective-permute-done.23.refs_4_), channel_id=1, source_target_pairs={{0,32},{8,40},{16,48},{24,56},{32,0},{40,8},{48,16},{56,24},{1,33}... | collective-permute-start | bytes 983048 | tf_op jit(solution)/shard_map/ppermute | solution.py:85
  233.9 12.1 %collective-permute-start.27 = (bf16[128,1280]{1,0:T(8,128)(2,1)S(1)}, bf16[128,1280]{1,0:T(8,128)(2,1)S(1)}, u32[]{:S(2)}, u32[]{:S(2)}) collective-permute-start(bf16[128,1280]{1,0:T(8,128)(2,1)S(1)} %collective-permute-done.23.refs_4_), channel_id=1, source_target_pairs={{0,48},{8,56},{16,0},{24,8},{32,16},{40,24},{48,32},{56,40},{1,49}... | collective-permute-start | bytes 983048 | tf_op jit(solution)/shard_map/ppermute | solution.py:85
  246.0 9.4 %collective-permute-start.30 = (bf16[2,144,256]{2,1,0:T(8,128)(2,1)S(1)}, bf16[2,144,256]{2,1,0:T(8,128)(2,1)S(1)}, u32[]{:S(2)}, u32[]{:S(2)}) collective-permute-start(bf16[2,144,256]{2,1,0:T(8,128)(2,1)S(1)} %pad_maximum_fusion.6), channel_id=1, source_target_pairs={{0,16},{8,24},{16,32},{24,40},{32,48},{40,56},{48,0},{56,8},{1,17}... | collective-permute-start | bytes 442376 | tf_op jit(solution)/shard_map/ppermute | solution.py:85
  246.7 8.7 %collective-permute-start.31 = (bf16[2,144,256]{2,1,0:T(8,128)(2,1)S(1)}, bf16[2,144,256]{2,1,0:T(8,128)(2,1)S(1)}, u32[]{:S(2)}, u32[]{:S(2)}) collective-permute-start(bf16[2,144,256]{2,1,0:T(8,128)(2,1)S(1)} %pad_maximum_fusion.6), channel_id=1, source_target_pairs={{0,32},{8,40},{16,48},{24,56},{32,0},{40,8},{48,16},{56,24},{1,33}... | collective-permute-start | bytes 442376 | tf_op jit(solution)/shard_map/ppermute | solution.py:85
  (51 other events, 692.7 us)
